TPU v7x, 32 devices: a whole 2x2x4 slice. The times are simulated.
32 devices in a mesh: seq: 8 (over z, y), chan: 4 (over x, core).
Axes of the slice: x: 2, y: 2, z: 4, core: 2. Of those that a mesh axis runs over, the one named last changes fastest.
Arguments:
- tokens: bfloat16 [4096, 8192], P('seq', 'chan'), may hold values from -6 to 6
- norm_gain: float32 [8192], replicated, may hold values from 0.1 to 1.9
- w_in: bfloat16 [8192, 3, 4096], P('seq', None, 'chan'), may hold values from -0.0625 to 0.0625
- short_taps: float32 [3, 3, 4096], P(None, None, 'chan'), may hold values from -3.6 to 3.6
- medium_taps: float32 [128, 256], P(None, 'chan'), may hold values from -0.75 to 0.75
- skip_gain: float32 [4096], P('chan'), may hold values from 0.5 to 1.5
- w_out: bfloat16 [4096, 8192], P('chan'), may hold values from -0.09375 to 0.09375
Outputs:
- block_out: bfloat16 [4096, 8192], P('seq', 'chan')
All inputs are finite; a program needn't handle non-finite values.
Results may differ from a plain program's by a relative error of at most 0.019.
Values may be sent and summed in bfloat16 or wider, within the bound.
No kernel may reach another device: no remote copies, remote signals or barrier semaphores. Data moves between devices by JAX's collectives and lax.ppermute only.
A program may use at most 192 MiB of HBM per device.

v0:
```python
import jax
import jax.numpy as jnp
from jax import lax
from jax.sharding import PartitionSpec as P

TAPS = 128
GROUP = 16


EPSILON = 1e-06


def passed_along(value, axis, steps):
    count = lax.axis_size(axis)
    first, last = (max(0, -steps), min(count, count - steps))
    return lax.ppermute(value, axis, [(source, source + steps) for source in range(first, last)])


def short_filter(extended, taps):
    return taps[0] * extended[2:] + taps[1] * extended[1:-1] + taps[2] * extended[:-2]


def per_device(tokens, norm_gain, w_in, short_taps, medium_taps, skip_gain, w_out):
    row_count = tokens.shape[0]
    channels = w_in.shape[2]
    gathered = lax.all_gather(tokens, "chan", axis=1, tiled=True)
    widened = gathered.astype(jnp.float32)
    mean_square = jnp.mean(widened * widened, axis=1, keepdims=True)
    normed = (widened * lax.rsqrt(mean_square + EPSILON) * norm_gain).astype(jnp.bfloat16)
    section = lax.all_gather(w_in, "seq", axis=0, tiled=True)
    flat_section = section.reshape(section.shape[0], 3 * channels)
    summed = jnp.dot(normed, flat_section, preferred_element_type=jnp.float32)
    projected = summed.astype(jnp.bfloat16).reshape(row_count, 3, channels)
    edge_rows = passed_along(projected[row_count - 2 :], "seq", 1)
    extended = lax.optimization_barrier(jnp.concatenate([edge_rows, projected], 0)).astype(
        jnp.float32
    )
    filtered = short_filter(extended, short_taps)
    queries = filtered[:, 0]
    product = (filtered[:, 1] * filtered[:, 2]).astype(jnp.bfloat16)
    product_rows = passed_along(product[row_count - (TAPS - 1) :], "seq", 1)
    reached = jnp.concatenate([product_rows, product], 0)
    floats = lax.optimization_barrier(reached).astype(jnp.float32)
    padded = jnp.concatenate([jnp.zeros((1, channels), jnp.float32), floats], 0)
    block_count = row_count // TAPS
    blocks = padded.reshape(block_count + 1, TAPS, channels)
    windows = jnp.concatenate([blocks[:-1], blocks[1:]], 1)
    cube_shape = (TAPS, TAPS, 2 * TAPS)
    lagged = (
        lax.broadcasted_iota(jnp.int32, cube_shape, 1)
        + TAPS
        - lax.broadcasted_iota(jnp.int32, cube_shape, 2)
    )
    onehot = (lagged == lax.broadcasted_iota(jnp.int32, cube_shape, 0)).astype(jnp.float32)
    toeplitz = jnp.einsum("jg,jis->gis", medium_taps, onehot, precision=lax.Precision.HIGHEST)
    filters = medium_taps.shape[1]
    grouped = windows.reshape(block_count, 2 * TAPS, filters, GROUP)
    convolved = jnp.einsum("gis,bsgc->bigc", toeplitz, grouped, precision=lax.Precision.HIGHEST)
    mixing = skip_gain * floats[TAPS - 1 :] + convolved.reshape(row_count, channels)
    gating = (queries * mixing).astype(jnp.bfloat16)
    partial_out = jnp.dot(gating, w_out, preferred_element_type=jnp.float32)
    rounded_out = lax.optimization_barrier(partial_out.astype(jnp.bfloat16)).astype(jnp.float32)
    projected_out = lax.psum_scatter(
        rounded_out.astype(jnp.bfloat16), "chan", scatter_dimension=1, tiled=True
    ).astype(jnp.float32)
    return (tokens.astype(jnp.float32) + projected_out).astype(jnp.bfloat16)


def solution(mesh):
    in_specs = (
        P("seq", "chan"),
        P(),
        P("seq", None, "chan"),
        P(None, None, "chan"),
        P(None, "chan"),
        P("chan"),
        P("chan", None),
    )
    out_specs = P("seq", "chan")
    return jax.shard_map(
        per_device, mesh=mesh, in_specs=in_specs, out_specs=out_specs, check_vma=False
    )
```

profile of v0, /device:TPU:4, one launch (start us, length us, event | category | flops | bytes accessed | tf_op | source)
XLA Modules:
  0.0 1216.3 jit_solution(826576138527569556)
XLA Ops:
  6.5 0.7 all-gather.3.cloned.1.call-update
  7.3 8.6 copy.10
  16.0 2.6 iota_compare_fusion
  18.6 11.1 fusion.3
  29.7 38.7 %all-gather.3.cloned.1.call-done = bf16[512,8192]{1,0:T(8,128)(2,1)} async-done(((bf16[512,2048]{1,0:T(8,128)(2,1)}), bf16[512,8192]{1,0:T(8,128)(2,1)}) %all-gather.3.cloned.1.call-update) | async-done | bytes 8388624 | tf_op jit(solution)/shard_map/all_gather | solution.py:26
  68.4 5.1 fusion
  73.6 947.7 %all-gather.5.cloned.1.call-done = bf16[8192,3,1024]{0,2,1:T(8,128)(2,1)} async-done(((bf16[1024,3,1024]{0,2,1:T(8,128)(2,1)}), bf16[8192,3,1024]{0,2,1:T(8,128)(2,1)}) %all-gather.5.cloned.1.call-update) | async-done | bytes 50331664 | tf_op jit(solution)/shard_map/all_gather | solution.py:30
  1021.2 33.1 %fusion.14 = bf16[512,3072]{1,0:T(8,128)(2,1)S(1)} fusion(bf16[8192,3072]{0,1:T(8,128)(2,1)} %bitcast.50, bf16[512,8192]{1,0:T(8,128)(2,1)} %all-gather.3.cloned.1.call-done, f32[8192]{0:T(1024)S(1)} %copy-done.7, f32[512]{0:T(512)S(1)} %add_rsqrt_fusion), kind=kOutput, calls=%fused_computation.20 | convolution fusion | flops 25788153856 | bytes 61900800 | tf_op jit(solution)/shard_map/dot_general | solution.py:32
  1054.4 4.5 collective-permute-start
  1058.9 3.4 copy.11
  1062.3 1.2 copy.12
  1063.5 3.2 pad_maximum_fusion
  1066.8 0.5 convert_element_type.43
  1067.3 5.6 fusion.12
  1072.9 0.4 fusion.22
  1073.4 3.1 collective-permute-start.1
  1076.4 0.4 fusion.35
  1076.8 6.5 collective-permute-done.1
  1083.3 0.7 pad_maximum_fusion.1
  1084.0 0.2 convert_element_type.46
  1084.1 1.8 slice.72
  1085.9 1.9 pad_slice_fusion
  1087.9 2.9 concatenate.20
  1090.8 3.1 copy.15
  1093.9 2.9 concatenate.21
  1096.8 1.9 copy.16
  1098.7 0.3 copy-done.4
  1099.0 16.3 %fusion.23 = f32[4,128,64,16]{1,3,0,2:T(8,128)S(1)} fusion(f32[128,256,64]{1,2,0:T(8,128)} %fusion.3, f32[4,128,64,16]{1,3,0,2:T(8,128)S(1)} %copy.16, f32[4,128,64,16]{1,3,0,2:T(8,128)S(1)} %copy-done.4), kind=kOutput, calls=%fused_computation.33 | convolution fusion | flops 1611661312 | bytes 14680064 | tf_op jit(solution)/shard_map/gis,bsgc->bigc/dot_general | solution.py:58
  1115.3 1.0 copy.17
  1116.3 17.9 %convolution_convert_fusion = bf16[512,8192]{1,0:T(8,128)(2,1)} fusion(bf16[1024,8192]{1,0:T(8,128)(2,1)} %param.13, f32[128,8,4,128]{3,2,1,0:T(4,128)S(1)} %bitcast.49, f32[512,3,1024]{0,2,1:T(8,128)} %copy-done.2, f32[1024]{0:T(1024)S(1)} %copy-done.8, f32[639,1024]{0,1:T(8,128)S(1)} %convert_element_type.46), kind=kOutput, calls=%fused_computation.8 | convolution fusion | flops 8596226048 | bytes 31461376 | tf_op jit(solution)/shard_map/dot_general | solution.py:61
  1134.3 71.8 %reduce-scatter.2.cloned.1.call-done = bf16[512,2048]{1,0:T(8,128)(2,1)} async-done(((bf16[512,8192]{1,0:T(8,128)(2,1)}), bf16[512,2048]{1,0:T(8,128)(2,1)}) %reduce-scatter.2.cloned.1.call-update) | async-done | bytes 2097168 | tf_op jit(solution)/shard_map/reduce_scatter | solution.py:63
  1206.1 3.7 add_convert_fusion
  (29 shorter events, 0.3 us)
Async XLA Ops:
  6.5 12.1 copy-start
  6.5 61.9 %all-gather.3.cloned.1.call-start = ((), (), s32[]{:S(2)}) async-start(), calls=%async_computation.1 | async-start | bytes 10485760 | tf_op jit(solution)/shard_map/all_gather | solution.py:26
  7.3 1014.0 %all-gather.5.cloned.1.call-start = ((), (), s32[]{:S(2)}) async-start(), calls=%async_computation.2 | async-start | bytes 56623104 | tf_op jit(solution)/shard_map/all_gather | solution.py:30
  16.0 1190.1 %reduce-scatter.2.cloned.1.call-start = ((), (), s32[]{:S(2)}) async-start(), calls=%async_computation.3 | async-start | bytes 10485760 | tf_op jit(solution)/shard_map/reduce_scatter | solution.py:63
  29.7 991.5 %copy-start.7 = (f32[8192]{0:T(1024)S(1)}, f32[8192]{0:T(1024)}, u32[]{:S(2)}) copy-start(f32[8192]{0:T(1024)} %param.8) | copy-start | bytes 98308
  1021.2 37.6 %copy-start.6 = (f32[3,3,1024]{2,1,0:T(4,128)S(1)}, f32[3,3,1024]{2,1,0:T(4,128)}, u32[]{:S(2)}) copy-start(f32[3,3,1024]{2,1,0:T(4,128)} %param.10) | copy-start | bytes 110596
  1054.3 4.5 copy-start.5
  1054.4 7.9 collective-permute-start
  1072.9 3.9 copy-start.2
  1073.4 9.9 collective-permute-start.1
  1096.8 2.2 copy-start.4
  1115.3 1.0 copy-start.8
  1134.3 71.8 %copy-start.3 = (bf16[512,2048]{1,0:T(8,128)(2,1)S(1)}, bf16[512,2048]{1,0:T(8,128)(2,1)}, u32[]{:S(2)}) copy-start(bf16[512,2048]{1,0:T(8,128)(2,1)} %param.7) | copy-start | bytes 6291460
  1134.3 75.5 %copy-start.1 = (f32[128,64]{0,1:T(8,128)S(1)}, f32[128,64]{0,1:T(8,128)}, u32[]{:S(2)}) copy-start(f32[128,64]{0,1:T(8,128)} %param.11) | copy-start | bytes 98308
Sparse Core Ops, SparseCore 0:
  8.9 59.4 all-gather.2
  70.0 951.1 all-gather.4
  1134.4 71.6 reduce-scatter.1
where the time goes:
time: 1220 us
  waiting for transfers between devices  1070 us (88%)
  matrix products  78.4 us (6%)
  local copies, waits for them, and re-layouts  29.3 us (2%)
  other arithmetic  22.3 us (2%)
  between operations  13.3 us (1%)
    all_gather x1, waiting for transfers between devices, per_device(): section = lax.all_gather(w_in, 'seq', axis=0, tiled=True)  948 us
    reduce_scatter x1, waiting for transfers between devices, per_device(): lax.psum_scatter(rounded_out.astype(jnp.bfloat16), 'chan', scatter_dimens...  71.8 us
    all_gather x1, waiting for transfers between devices, per_device(): gathered = lax.all_gather(tokens, 'chan', axis=1, tiled=True)  38.7 us
    dot_general x1, matrix products, per_device(): summed = jnp.dot(normed, flat_section, preferred_element_type=jnp.float32)  33.1 us
  transfers between devices with their start and end apart: 5, of which 4 were waited for; matrix products, arithmetic and copies ran while one was open for 3% of the time, Pallas kernels for 0%

commit v1 on v0

v1 whole, which is shorter than its diff:
```python
import jax
import jax.numpy as jnp
from jax import lax
from jax.sharding import PartitionSpec as P

TAPS = 128
GROUP = 16
PIECES = 4
EPSILON = 1e-06


def passed_along(value, axis, steps):
    count = lax.axis_size(axis)
    first, last = (max(0, -steps), min(count, count - steps))
    return lax.ppermute(value, axis, [(source, source + steps) for source in range(first, last)])


def swapped(value, axis, bit):
    return lax.ppermute(value, axis, [(i, i ^ bit) for i in range(lax.axis_size(axis))])


def short_filter(extended, taps):
    return taps[0] * extended[2:] + taps[1] * extended[1:-1] + taps[2] * extended[:-2]


def spread_tokens(tokens, norm_gain):
    seq, chan = lax.axis_size("seq"), lax.axis_size("chan")
    layers = seq // 2
    groups = [list(range(start, seq, 2)) for start in range(2)]
    odd = lax.axis_index("seq") % 2 == 1
    whole = lax.all_to_all(tokens, "chan", 0, 1, tiled=True)
    widened = whole.astype(jnp.float32)
    mean_square = jnp.mean(widened * widened, axis=1, keepdims=True)
    normed = (widened * lax.rsqrt(mean_square + EPSILON) * norm_gain).astype(jnp.bfloat16)
    rows, depth = normed.shape
    halves = normed.reshape(rows, layers, 2, depth // seq)
    halves = jnp.where(odd, halves[:, :, ::-1], halves).reshape(rows, depth)
    shared = lax.all_to_all(halves, "seq", 1, 0, axis_index_groups=groups, tiled=True)
    shared = shared.reshape(layers, rows, depth // layers)
    return lax.all_gather(shared, "chan", axis=1, tiled=True)


def toeplitz_of(medium_taps):
    cube_shape = (TAPS, TAPS, 2 * TAPS)
    lagged = (
        lax.broadcasted_iota(jnp.int32, cube_shape, 1)
        + TAPS
        - lax.broadcasted_iota(jnp.int32, cube_shape, 2)
    )
    onehot = (lagged == lax.broadcasted_iota(jnp.int32, cube_shape, 0)).astype(jnp.bfloat16)
    return jnp.einsum("jg,jis->gis", medium_taps.astype(jnp.bfloat16), onehot)


def mixed(projected, short_taps, toeplitz, skip_gain):
    row_count, _, channels = projected.shape
    edge_rows = passed_along(projected[row_count - 2 :], "seq", 1)
    extended = jnp.concatenate([edge_rows, projected], 0).astype(jnp.float32)
    filtered = short_filter(extended, short_taps)
    queries = filtered[:, 0]
    product = (filtered[:, 1] * filtered[:, 2]).astype(jnp.bfloat16)
    product_rows = passed_along(product[row_count - TAPS :], "seq", 1)
    padded = jnp.concatenate([product_rows, product], 0)
    block_count = row_count // TAPS
    blocks = padded.reshape(block_count + 1, TAPS, channels)
    windows = jnp.concatenate([blocks[:-1], blocks[1:]], 1)
    filters = channels // GROUP
    grouped = windows.reshape(block_count, 2 * TAPS, filters, GROUP)
    convolved = jnp.einsum("gis,bsgc->bigc", toeplitz, grouped, preferred_element_type=jnp.float32)
    mixing = skip_gain * product.astype(jnp.float32) + convolved.reshape(row_count, channels)
    return (queries * mixing).astype(jnp.bfloat16)


def per_device(tokens, norm_gain, w_in, short_taps, medium_taps, skip_gain, w_out):
    seq, chan = lax.axis_size("seq"), lax.axis_size("chan")
    layers = seq // 2
    groups = [list(range(start, seq, 2)) for start in range(2)]
    row_count = tokens.shape[0]
    channels = w_in.shape[2]
    width = channels // PIECES
    pieces = [w_in[:, :, i * width : (i + 1) * width] for i in range(PIECES)]
    pieces = [piece.reshape(piece.shape[0], 3 * width) for piece in pieces]
    others = [swapped(piece, "seq", 1) for piece in pieces]
    spread = spread_tokens(tokens, norm_gain)
    spread = spread.reshape(layers * row_count, spread.shape[2])
    toeplitz = toeplitz_of(medium_taps)
    filters = width // GROUP
    gates = []
    for i in range(PIECES):
        section = jnp.concatenate([pieces[i], others[i]], 0)
        summed = jnp.dot(spread, section, preferred_element_type=jnp.float32).astype(jnp.bfloat16)
        projected = lax.psum_scatter(
            summed, "seq", scatter_dimension=0, axis_index_groups=groups, tiled=True
        )
        span = slice(i * width, (i + 1) * width)
        gates.append(
            mixed(
                projected.reshape(row_count, 3, width),
                short_taps[:, :, span],
                toeplitz[i * filters : (i + 1) * filters],
                skip_gain[span],
            )
        )
    gating = jnp.concatenate(gates, 1)
    partial_out = jnp.dot(gating, w_out, preferred_element_type=jnp.float32).astype(jnp.bfloat16)
    projected_out = lax.psum_scatter(partial_out, "chan", scatter_dimension=1, tiled=True)
    return (tokens.astype(jnp.float32) + projected_out.astype(jnp.float32)).astype(jnp.bfloat16)


def solution(mesh):
    in_specs = (
        P("seq", "chan"),
        P(),
        P("seq", None, "chan"),
        P(None, None, "chan"),
        P(None, "chan"),
        P("chan"),
        P("chan", None),
    )
    out_specs = P("seq", "chan")
    return jax.shard_map(
        per_device, mesh=mesh, in_specs=in_specs, out_specs=out_specs, check_vma=False
    )
```

time: 1220 us -> 645 us (0.53)
  waiting for transfers between devices: 1070 us -> 340 us
  local copies, waits for them, and re-layouts: 29.3 us -> 90.5 us
  blocking collectives: 0 us -> 52.8 us
  starting transfers between devices: 7.61 us -> 31 us
  other arithmetic: 22.3 us -> 35.7 us
    all_gather x2 -> x1, waiting for transfers between devices: 986 us -> 13.9 us  [spread_tokens(): return lax.all_gather(shared, 'chan', axis=1, tiled=True)]
    ppermute x0 -> x4, waiting for transfers between devices: none -> 141 us  [swapped(): lax.ppermute(value, axis, [(i, i ^ bit) for i in range(lax.axis_size(axis...]
    reduce_scatter x1 -> x5, waiting for transfers between devices: 71.8 us -> 159 us  [the longest x4 88.9 us: per_device(): lax.psum_scatter(summed, 'seq', scatter_dimension=0, axis_index_groups=gr...]
    all_to_all x0 -> x1, blocking collectives: none -> 52.8 us  [spread_tokens(): lax.all_to_all(halves, 'seq', 1, 0, axis_index_groups=groups, tiled=True)]
    all_to_all x0 -> x1, waiting for transfers between devices: none -> 25.6 us  [spread_tokens(): whole = lax.all_to_all(tokens, 'chan', 0, 1, tiled=True)]
    rev x0 -> x1, local copies, waits for them, and re-layouts: none -> 18.4 us  [spread_tokens(): halves = jnp.where(odd, halves[:, :, ::-1], halves).reshape(rows, depth)]
    convert_element_type x1 -> x10, local copies, waits for them, and re-layouts: 3.41 us -> 20.4 us  [the longest x9 13.8 us: mixed(): product = (filtered[:, 1] * filtered[:, 2]).astype(jnp.bfloat16)]
    ppermute x2 -> x8, starting transfers between devices: 7.53 us -> 24.3 us  [passed_along(): lax.ppermute(value, axis, [(source, source + steps) for source in range(f...]
  transfers between devices with their start and end apart: 5 -> 19, of which waited for: 4 -> 9; matrix products, arithmetic and copies ran while one was open for 3% -> 18% of each run, Pallas kernels for 0% -> 0%
where the time goes in v1:
time: 645 us; the launch traced here: 633 us
  waiting for transfers between devices  340 us (53%)
  local copies, waits for them, and re-layouts  90.5 us (14%)
  matrix products  68.9 us (11%)
  blocking collectives  52.8 us (8%)
  other arithmetic  35.7 us (6%)
  starting transfers between devices  31 us (5%)
  between operations  14.6 us (2%)
    ppermute x4, waiting for transfers between devices, swapped(): lax.ppermute(value, axis, [(i, i ^ bit) for i in range(lax.axis_size(axis...  141 us
    reduce_scatter x4, waiting for transfers between devices, per_device(): lax.psum_scatter(summed, 'seq', scatter_dimension=0, axis_index_groups=gr...  88.9 us
    reduce_scatter x1, waiting for transfers between devices, per_device(): lax.psum_scatter(partial_out, 'chan', scatter_dimension=1, tiled=True)  70.3 us
    all_to_all x1, blocking collectives, spread_tokens(): lax.all_to_all(halves, 'seq', 1, 0, axis_index_groups=groups, tiled=True)  52.8 us
    dot_general x4, matrix products, per_device(): jnp.dot(spread, section, preferred_element_type=jnp.float32)  43 us
    all_to_all x1, waiting for transfers between devices, spread_tokens(): whole = lax.all_to_all(tokens, 'chan', 0, 1, tiled=True)  25.6 us
    ppermute x8, starting transfers between devices, passed_along(): lax.ppermute(value, axis, [(source, source + steps) for source in range(f...  24.3 us
    rev x1, local copies, waits for them, and re-layouts, spread_tokens(): halves = jnp.where(odd, halves[:, :, ::-1], halves).reshape(rows, depth)  18.4 us
  transfers between devices with their start and end apart: 19, of which 9 were waited for; matrix products, arithmetic and copies ran while one was open for 18% of the time, Pallas kernels for 0%

profile of v1, /device:TPU:4, one launch (start us, length us, event | category | flops | bytes accessed | tf_op | source)
XLA Modules:
  0.0 633.0 jit_solution(15094682864922985278)
XLA Ops:
  6.5 3.7 all-to-all-start
  10.4 25.6 %all-to-all-done = bf16[4,128,2048]{2,1,0:T(8,128)(2,1)S(1)} async-done(((bf16[4,128,2048]{2,1,0:T(8,128)(2,1)}), bf16[4,128,2048]{2,1,0:T(8,128)(2,1)S(1)}, u32[]{:S(2)}, u32[]{:S(2)}) %all-to-all-start) | async-done | bytes 2097184 | tf_op jit(solution)/shard_map/all_to_all | solution.py:31
  38.5 6.6 %reshape.153 = f32[128,4,2,1024]{3,2,0,1:T(2,128)} reshape(f32[128,4,2048]{2,0,1:T(8,128)} %convert_bitcast_fusion) | data formatting | bytes 8388608 | tf_op jit(solution)/shard_map/convert_element_type | solution.py:32
  45.6 5.5 multiply_convert_fusion
  51.1 18.4 %rev.3 = bf16[128,4,2,1024]{3,2,0,1:T(2,128)(2,1)S(1)} reverse(bf16[128,4,2,1024]{3,2,0,1:T(2,128)(2,1)} %multiply_convert_fusion), dimensions={2} | reverse | bytes 4194304 | tf_op jit(solution)/shard_map/rev | solution.py:37
  69.5 6.5 %broadcast_select_fusion = bf16[128,4,2,1024]{3,2,0,1:T(2,128)(2,1)} fusion(bf16[128,4,2,1024]{3,2,0,1:T(2,128)(2,1)S(1)} %rev.3, pred[]{:T(512)S(6)} %eq.8, f32[4,2,1024]{2,1,0:T(2,128)S(1)} %mul.218, f32[128,4,2,1024]{3,2,0,1:T(2,128)} %reshape.153, f32[128]{0:T(128)S(1)} %add_rsqrt_fusion), kind=kLoop, calls=%fused_computation.9 | loop fusion | flops 4194304 | bytes 8421889 | tf_op jit(solution)/shard_map/jit(_where)/select_n | solution.py:37
  76.0 3.3 all_to_all.24
  79.3 52.8 %all_to_all.29 = bf16[128,4,2048]{2,0,1:T(8,128)(2,1)} all-to-all(bf16[128,4,2048]{2,0,1:T(8,128)(2,1)S(1)} %all_to_all.24), channel_id=1, replica_groups={{0,8,16,24},{4,12,20,28},{1,9,17,25},{5,13,21,29},{2,10,18,26},{6,14,22..., dimensions={1} | all-to-all | bytes 4194304 | tf_op jit(solution)/shard_map/all_to_all | solution.py:38
  132.2 5.0 fusion.70
  137.1 2.7 copy.70
  140.4 34.6 %collective-permute-done.9 = bf16[1024,768]{0,1:T(8,128)(2,1)} collective-permute-done((bf16[1024,768]{0,1:T(8,128)(2,1)}, bf16[1024,768]{0,1:T(8,128)(2,1)}, u32[]{:S(2)}, u32[]{:S(2)}) %collective-permute-start.9) | collective-permute-done | bytes 1572896 | tf_op jit(solution)/shard_map/ppermute | solution.py:19
  175.0 13.9 %all-gather.2.cloned.1.call-done = bf16[4,512,2048]{2,1,0:T(8,128)(2,1)} async-done(((bf16[4,128,2048]{2,1,0:T(8,128)(2,1)}), bf16[4,512,2048]{2,1,0:T(8,128)(2,1)}) %all-gather.2.cloned.1.call-update) | async-done | bytes 8388624 | tf_op jit(solution)/shard_map/all_gather | solution.py:40
  188.9 11.2 %convolution_convert_fusion.1 = bf16[2048,768]{1,0:T(8,128)(2,1)} fusion(bf16[2048,2048]{1,0:T(8,128)(2,1)} %bitcast.181, bf16[1024,768]{0,1:T(8,128)(2,1)} %collective-permute-done.9, bf16[1024,768]{0,1:T(8,128)(2,1)} %bitcast.172), kind=kOutput, calls=%fused_computation.10 | convolution fusion | flops 6450315264 | bytes 14680064 | tf_op jit(solution)/shard_map/dot_general | solution.py:90
  200.4 2.6 copy.69
  203.6 36.2 %collective-permute-done.6 = bf16[1024,768]{0,1:T(8,128)(2,1)S(1)} collective-permute-done((bf16[1024,768]{0,1:T(8,128)(2,1)}, bf16[1024,768]{0,1:T(8,128)(2,1)S(1)}, u32[]{:S(2)}, u32[]{:S(2)}) %collective-permute-start.6) | collective-permute-done | bytes 1572896 | tf_op jit(solution)/shard_map/ppermute | solution.py:19
  239.8 10.8 %convolution_convert_fusion.2 = bf16[2048,768]{1,0:T(8,128)(2,1)} fusion(bf16[2048,2048]{1,0:T(8,128)(2,1)} %bitcast.182, bf16[1024,768]{0,1:T(8,128)(2,1)S(1)} %collective-permute-done.6, bf16[1024,768]{0,1:T(8,128)(2,1)} %bitcast.176), kind=kOutput, calls=%fused_computation.11 | convolution fusion | flops 6450315264 | bytes 14680064 | tf_op jit(solution)/shard_map/dot_general | solution.py:90
  253.0 35.5 %collective-permute-done.3 = bf16[1024,768]{0,1:T(8,128)(2,1)S(1)} collective-permute-done((bf16[1024,768]{0,1:T(8,128)(2,1)}, bf16[1024,768]{0,1:T(8,128)(2,1)S(1)}, u32[]{:S(2)}, u32[]{:S(2)}) %collective-permute-start.3) | collective-permute-done | bytes 1572896 | tf_op jit(solution)/shard_map/ppermute | solution.py:19
  288.5 10.7 %convolution_convert_fusion.3 = bf16[2048,768]{1,0:T(8,128)(2,1)} fusion(bf16[2048,2048]{1,0:T(8,128)(2,1)} %bitcast.183, bf16[1024,768]{0,1:T(8,128)(2,1)S(1)} %collective-permute-done.3, bf16[1024,768]{0,1:T(8,128)(2,1)} %bitcast.178), kind=kOutput, calls=%fused_computation.12 | convolution fusion | flops 6450315264 | bytes 14680064 | tf_op jit(solution)/shard_map/dot_general | solution.py:90
  300.8 34.5 %collective-permute-done = bf16[1024,768]{0,1:T(8,128)(2,1)S(1)} collective-permute-done((bf16[1024,768]{0,1:T(8,128)(2,1)S(1)}, bf16[1024,768]{0,1:T(8,128)(2,1)S(1)}, u32[]{:S(2)}, u32[]{:S(2)}) %collective-permute-start) | collective-permute-done | bytes 1572896 | tf_op jit(solution)/shard_map/ppermute | solution.py:19
  335.3 10.3 %convolution_convert_fusion.4 = bf16[2048,768]{1,0:T(8,128)(2,1)} fusion(bf16[2048,2048]{1,0:T(8,128)(2,1)} %bitcast.184, bf16[1024,768]{0,1:T(8,128)(2,1)S(1)} %collective-permute-done, bf16[1024,768]{0,1:T(8,128)(2,1)S(1)} %bitcast.174), kind=kOutput, calls=%fused_computation.13 | convolution fusion | flops 6450315264 | bytes 14680064 | tf_op jit(solution)/shard_map/dot_general | solution.py:90
  347.0 4.1 fusion.15
  354.9 3.4 collective-permute-start.10
  360.6 3.4 collective-permute-start.7
  363.9 28.2 %reduce-scatter.8.cloned.1.call-done = bf16[512,768]{1,0:T(8,128)(2,1)} async-done(((bf16[2048,768]{1,0:T(8,128)(2,1)}), bf16[512,768]{1,0:T(8,128)(2,1)}) %reduce-scatter.8.cloned.1.call-update) | async-done | bytes 786448 | tf_op jit(solution)/shard_map/reduce_scatter | solution.py:91
  395.7 60.7 %reduce-scatter.6.cloned.1.call-done = bf16[512,768]{1,0:T(8,128)(2,1)} async-done(((bf16[2048,768]{1,0:T(8,128)(2,1)}), bf16[512,768]{1,0:T(8,128)(2,1)}) %reduce-scatter.6.cloned.1.call-update) | async-done | bytes 786448 | tf_op jit(solution)/shard_map/reduce_scatter | solution.py:91
  457.6 2.9 collective-permute-start.1
  475.8 3.4 collective-permute-start.11
  496.7 3.9 collective-permute-start.8
  502.4 3.4 collective-permute-start.5
  534.7 17.0 %convolution_convert_fusion = bf16[512,8192]{1,0:T(8,128)(2,1)} fusion(bf16[1024,8192]{1,0:T(8,128)(2,1)} %param.13, bf16[512,256]{0,1:T(8,128)(2,1)S(1)} %get-tuple-element.29, bf16[512,256]{0,1:T(8,128)(2,1)S(1)} %get-tuple-element.30, bf16[512,256]{0,1:T(8,128)(2,1)S(1)} %get-tuple-element.31, bf16[512,256]{0,1:T(8,128)(2,1)S(1)} %get-tuple-element.32), kind=kOutput, calls=%fused_computation.2 | convolution fusion | flops 8598323200 | bytes 26214400 | tf_op jit(solution)/shard_map/dot_general | solution.py:104
  551.7 70.3 %reduce-scatter.14.cloned.1.call-done = bf16[512,2048]{1,0:T(8,128)(2,1)} async-done(((bf16[512,8192]{1,0:T(8,128)(2,1)}), bf16[512,2048]{1,0:T(8,128)(2,1)}) %reduce-scatter.14.cloned.1.call-update) | async-done | bytes 2097168 | tf_op jit(solution)/shard_map/reduce_scatter | solution.py:105
  622.1 3.7 add_convert_fusion
  (179 shorter events, 83.6 us)
Async XLA Ops:
  6.5 3.8 copy-start.23
  6.5 29.4 %all-to-all-start = ((bf16[4,128,2048]{2,1,0:T(8,128)(2,1)}), bf16[4,128,2048]{2,1,0:T(8,128)(2,1)S(1)}, u32[]{:S(2)}, u32[]{:S(2)}) async-start(bf16[4,128,2048]{2,1,0:T(8,128)(2,1)} %bitcast.161), calls=%async_computation | async-start | bytes 4194304 | tf_op jit(solution)/shard_map/all_to_all | solution.py:31
  10.3 178.6 %all-gather.2.cloned.1.call-start = ((), (), s32[]{:S(2)}) async-start(), calls=%async_computation.7 | async-start | bytes 10485760 | tf_op jit(solution)/shard_map/all_gather | solution.py:40
  132.1 221.2 %reduce-scatter.12.cloned.1.call-start = ((), (), s32[]{:S(2)}) async-start(), calls=%async_computation.11 | async-start | bytes 3932160 | tf_op jit(solution)/shard_map/reduce_scatter | solution.py:91
  139.9 35.1 %collective-permute-start.9 = (bf16[1024,768]{0,1:T(8,128)(2,1)}, bf16[1024,768]{0,1:T(8,128)(2,1)}, u32[]{:S(2)}, u32[]{:S(2)}) collective-permute-start(bf16[1024,768]{0,1:T(8,128)(2,1)} %bitcast.171), channel_id=1, source_target_pairs={{0,4},{4,0},{8,12},{12,8},{16,20},{20,16},{24,28},{28,24},{1,5},{5... | collective-permute-start | bytes 4718600 | tf_op jit(solution)/shard_map/ppermute | solution.py:19
  200.2 158.7 %reduce-scatter.10.cloned.1.call-start = ((), (), s32[]{:S(2)}) async-start(), calls=%async_computation.10 | async-start | bytes 3932160 | tf_op jit(solution)/shard_map/reduce_scatter | solution.py:91
  203.1 36.8 %collective-permute-start.6 = (bf16[1024,768]{0,1:T(8,128)(2,1)}, bf16[1024,768]{0,1:T(8,128)(2,1)S(1)}, u32[]{:S(2)}, u32[]{:S(2)}) collective-permute-start(bf16[1024,768]{0,1:T(8,128)(2,1)} %bitcast.175), channel_id=1, source_target_pairs={{0,4},{4,0},{8,12},{12,8},{16,20},{20,16},{24,28},{28,24},{1,5},{5... | collective-permute-start | bytes 4718600 | tf_op jit(solution)/shard_map/ppermute | solution.py:19
  250.6 141.5 %reduce-scatter.8.cloned.1.call-start = ((), (), s32[]{:S(2)}) async-start(), calls=%async_computation.9 | async-start | bytes 3932160 | tf_op jit(solution)/shard_map/reduce_scatter | solution.py:91
  252.4 36.1 %collective-permute-start.3 = (bf16[1024,768]{0,1:T(8,128)(2,1)}, bf16[1024,768]{0,1:T(8,128)(2,1)S(1)}, u32[]{:S(2)}, u32[]{:S(2)}) collective-permute-start(bf16[1024,768]{0,1:T(8,128)(2,1)} %bitcast.177), channel_id=1, source_target_pairs={{0,4},{4,0},{8,12},{12,8},{16,20},{20,16},{24,28},{28,24},{1,5},{5... | collective-permute-start | bytes 4718600 | tf_op jit(solution)/shard_map/ppermute | solution.py:19
  299.2 157.1 %reduce-scatter.6.cloned.1.call-start = ((), (), s32[]{:S(2)}) async-start(), calls=%async_computation.8 | async-start | bytes 3932160 | tf_op jit(solution)/shard_map/reduce_scatter | solution.py:91
  300.2 35.1 %collective-permute-start = (bf16[1024,768]{0,1:T(8,128)(2,1)S(1)}, bf16[1024,768]{0,1:T(8,128)(2,1)S(1)}, u32[]{:S(2)}, u32[]{:S(2)}) collective-permute-start(bf16[1024,768]{0,1:T(8,128)(2,1)S(1)} %bitcast.173), channel_id=1, source_target_pairs={{0,4},{4,0},{8,12},{12,8},{16,20},{20,16},{24,28},{28,24},{1,5},{5... | collective-permute-start | bytes 4718600 | tf_op jit(solution)/shard_map/ppermute | solution.py:19
  345.6 276.5 %reduce-scatter.14.cloned.1.call-start = ((), (), s32[]{:S(2)}) async-start(), calls=%async_computation.12 | async-start | bytes 10485760 | tf_op jit(solution)/shard_map/reduce_scatter | solution.py:105
  351.2 7.1 %copy-start.32 = (f32[1024]{0:T(1024)S(1)}, f32[1024]{0:T(1024)}, u32[]{:S(2)}) copy-start(f32[1024]{0:T(1024)} %param.12) | copy-start | bytes 12292
  354.9 109.7 %collective-permute-start.10 = (bf16[2,3,256]{0,2,1:T(8,128)(2,1)}, bf16[2,3,256]{0,2,1:T(8,128)(2,1)S(1)}, u32[]{:S(2)}, u32[]{:S(2)}) collective-permute-start(bf16[2,3,256]{0,2,1:T(8,128)(2,1)} %bitcast.41), channel_id=1, source_target_pairs={{0,4},{4,8},{8,12},{12,16},{16,20},{20,24},{24,28},{1,5},{5,9},{9,... | collective-permute-start | bytes 9224 | tf_op jit(solution)/shard_map/ppermute | solution.py:15
  358.9 103.0 %copy-start.16 = (bf16[512,768]{1,0:T(8,128)(2,1)S(1)}, bf16[512,768]{1,0:T(8,128)(2,1)}, u32[]{:S(2)}) copy-start(bf16[512,768]{1,0:T(8,128)(2,1)} %reduce-scatter.10.cloned.1.call-done) | copy-start | bytes 2359300
  360.6 106.8 %collective-permute-start.7 = (bf16[2,3,256]{0,2,1:T(8,128)(2,1)}, bf16[2,3,256]{0,2,1:T(8,128)(2,1)}, u32[]{:S(2)}, u32[]{:S(2)}) collective-permute-start(bf16[2,3,256]{0,2,1:T(8,128)(2,1)} %bitcast.30), channel_id=1, source_target_pairs={{0,4},{4,8},{8,12},{12,16},{16,20},{20,24},{24,28},{1,5},{5,9},{9,... | collective-permute-start | bytes 9224 | tf_op jit(solution)/shard_map/ppermute | solution.py:15
  392.1 70.1 %copy-start.17 = (bf16[512,768]{1,0:T(8,128)(2,1)S(1)}, bf16[512,768]{1,0:T(8,128)(2,1)}, u32[]{:S(2)}) copy-start(bf16[512,768]{1,0:T(8,128)(2,1)} %reduce-scatter.8.cloned.1.call-done) | copy-start | bytes 2359300
  393.8 77.2 %collective-permute-start.4 = (bf16[2,3,256]{0,2,1:T(8,128)(2,1)}, bf16[2,3,256]{0,2,1:T(8,128)(2,1)S(1)}, u32[]{:S(2)}, u32[]{:S(2)}) collective-permute-start(bf16[2,3,256]{0,2,1:T(8,128)(2,1)} %bitcast.19), channel_id=1, source_target_pairs={{0,4},{4,8},{8,12},{12,16},{16,20},{20,24},{24,28},{1,5},{5,9},{9,... | collective-permute-start | bytes 9224 | tf_op jit(solution)/shard_map/ppermute | solution.py:15
  457.6 22.2 %collective-permute-start.1 = (bf16[2,3,256]{2,1,0:T(4,128)(2,1)}, bf16[2,3,256]{2,1,0:T(4,128)(2,1)}, u32[]{:S(2)}, u32[]{:S(2)}) collective-permute-start(bf16[2,3,256]{2,1,0:T(4,128)(2,1)} %slice.235), channel_id=1, source_target_pairs={{0,4},{4,8},{8,12},{12,16},{16,20},{20,24},{24,28},{1,5},{5,9},{9,... | collective-permute-start | bytes 9224 | tf_op jit(solution)/shard_map/ppermute | solution.py:15
  466.5 8.7 %copy-start.9 = (bf16[512,1,256]{0,2,1:T(8,128)(2,1)}, bf16[512,1,256]{0,2,1:T(8,128)(2,1)S(1)}, u32[]{:S(2)}) copy-start(bf16[512,1,256]{0,2,1:T(8,128)(2,1)S(1)} %fusion.43) | copy-start | bytes 786436
  470.2 9.1 %copy-start.10 = (bf16[512,1,256]{0,2,1:T(8,128)(2,1)}, bf16[512,1,256]{0,2,1:T(8,128)(2,1)S(1)}, u32[]{:S(2)}) copy-start(bf16[512,1,256]{0,2,1:T(8,128)(2,1)S(1)} %fusion.44) | copy-start | bytes 786436
  475.8 34.5 %collective-permute-start.11 = (bf16[128,256]{0,1:T(8,128)(2,1)}, bf16[128,256]{0,1:T(8,128)(2,1)S(1)}, u32[]{:S(2)}, u32[]{:S(2)}) collective-permute-start(bf16[128,256]{0,1:T(8,128)(2,1)} %slice_bitcast_fusion.8), channel_id=1, source_target_pairs={{0,4},{4,8},{8,12},{12,16},{16,20},{20,24},{24,28},{1,5},{5,9},{9,... | collective-permute-start | bytes 196616 | tf_op jit(solution)/shard_map/ppermute | solution.py:15
  493.2 17.1 %copy-start.11 = (bf16[512,256]{0,1:T(8,128)(2,1)S(1)}, bf16[512,256]{0,1:T(8,128)(2,1)}, u32[]{:S(2)}) copy-start(bf16[512,256]{0,1:T(8,128)(2,1)} %fusion.79) | copy-start | bytes 786436
  496.7 17.8 %collective-permute-start.8 = (bf16[128,256]{0,1:T(8,128)(2,1)}, bf16[128,256]{0,1:T(8,128)(2,1)}, u32[]{:S(2)}, u32[]{:S(2)}) collective-permute-start(bf16[128,256]{0,1:T(8,128)(2,1)} %slice_bitcast_fusion.9), channel_id=1, source_target_pairs={{0,4},{4,8},{8,12},{12,16},{16,20},{20,24},{24,28},{1,5},{5,9},{9,... | collective-permute-start | bytes 196616 | tf_op jit(solution)/shard_map/ppermute | solution.py:15
  502.4 17.3 %collective-permute-start.5 = (bf16[128,256]{0,1:T(8,128)(2,1)}, bf16[128,256]{0,1:T(8,128)(2,1)}, u32[]{:S(2)}, u32[]{:S(2)}) collective-permute-start(bf16[128,256]{0,1:T(8,128)(2,1)} %slice_bitcast_fusion.10), channel_id=1, source_target_pairs={{0,4},{4,8},{8,12},{12,16},{16,20},{20,24},{24,28},{1,5},{5,9},{9,... | collective-permute-start | bytes 196616 | tf_op jit(solution)/shard_map/ppermute | solution.py:15
  508.2 20.2 %collective-permute-start.2 = (bf16[128,256]{1,0:T(8,128)(2,1)}, bf16[128,256]{1,0:T(8,128)(2,1)S(1)}, u32[]{:S(2)}, u32[]{:S(2)}) collective-permute-start(bf16[128,256]{1,0:T(8,128)(2,1)} %bitcast.180), channel_id=1, source_target_pairs={{0,4},{4,8},{8,12},{12,16},{16,20},{20,24},{24,28},{1,5},{5,9},{9,... | collective-permute-start | bytes 196616 | tf_op jit(solution)/shard_map/ppermute | solution.py:15
  511.1 8.6 %copy-start.12 = (bf16[512,256]{0,1:T(8,128)(2,1)S(1)}, bf16[512,256]{0,1:T(8,128)(2,1)}, u32[]{:S(2)}) copy-start(bf16[512,256]{0,1:T(8,128)(2,1)} %fusion.77) | copy-start | bytes 786436
  522.3 2.5 copy-start.14
  525.4 3.0 copy-start.13
  529.3 3.2 copy-start.35
  529.3 3.2 copy-start.36
  551.7 70.4 %copy-start.4 = (bf16[512,2048]{1,0:T(8,128)(2,1)S(1)}, bf16[512,2048]{1,0:T(8,128)(2,1)}, u32[]{:S(2)}) copy-start(bf16[512,2048]{1,0:T(8,128)(2,1)} %param.7) | copy-start | bytes 6291460
  (25 other events, 44.1 us)
Sparse Core Ops, SparseCore 0:
  132.2 56.6 all-gather.1
  200.3 60.2 reduce-scatter.11
  262.9 60.2 reduce-scatter.9
  325.4 66.7 reduce-scatter.7
  394.3 62.0 reduce-scatter.5
  551.9 70.1 reduce-scatter.13

commit v2 on v0

v2 whole, which is shorter than its diff:
```python
import jax
import jax.numpy as jnp
from jax import lax
from jax.experimental import pallas as pl
from jax.experimental.pallas import tpu as pltpu
from jax.sharding import PartitionSpec as P

TAPS = 128
GROUP = 16
EDGE = TAPS + 16
PARTS = 2
EPSILON = 1e-06


def swapped(value, axis, bit):
    return lax.ppermute(value, axis, [(i, i ^ bit) for i in range(lax.axis_size(axis))])


def project(order, rows, sections, addend):
    count, depth = rows.shape
    step, width = sections[0].shape
    tile = min(count, 256)

    def kernel(order_ref, rows_ref, *refs):
        total = jnp.zeros((tile, width), jnp.float32)
        for i in range(len(sections)):
            place = pl.ds(pl.multiple_of(order_ref[i] * step, step), step)
            total += jnp.dot(rows_ref[:, place], refs[i][...], preferred_element_type=jnp.float32)
        if addend is not None:
            total += refs[len(sections)][...].astype(jnp.float32)
        refs[-1][...] = total.astype(jnp.bfloat16)

    whole = pl.BlockSpec((step, width), lambda i, _: (0, 0))
    piece = pl.BlockSpec((tile, width), lambda i, _: (i, 0))
    extra = [] if addend is None else [addend]
    return pl.pallas_call(
        kernel,
        grid_spec=pltpu.PrefetchScalarGridSpec(
            num_scalar_prefetch=1,
            grid=(count // tile,),
            in_specs=[pl.BlockSpec((tile, depth), lambda i, _: (i, 0))]
            + [whole] * len(sections)
            + [piece] * len(extra),
            out_specs=piece,
        ),
        out_shape=jax.ShapeDtypeStruct((count, width), jnp.bfloat16),
        compiler_params=pltpu.CompilerParams(vmem_limit_bytes=40 << 20),
        cost_estimate=pl.CostEstimate(
            flops=2 * count * depth * width,
            bytes_accessed=2 * (count * depth + depth * width + count * width),
            transcendentals=0,
        ),
        name="project",
    )(order, rows, *sections, *extra)


def gate(halo, parts, short_taps, skip_gain, toeplitz):
    slots, part_rows, wide = parts[0].shape
    width = wide // 3
    row_count = part_rows * len(parts)
    filters = toeplitz.shape[1] // (2 * TAPS)

    def kernel(halo_ref, *refs):
        part_refs = refs[: len(parts)]
        taps_ref, skip_ref, toeplitz_ref, out_ref, extended = refs[len(parts) :]
        extended[:EDGE] = halo_ref[0].astype(jnp.float32)
        for i, ref in enumerate(part_refs):
            extended[EDGE + i * part_rows : EDGE + (i + 1) * part_rows] = ref[0].astype(jnp.float32)
        rows = TAPS + row_count
        filtered = sum(
            taps_ref[lag : lag + 1] * extended[16 - lag : 16 - lag + rows] for lag in range(3)
        )
        product = filtered[:, width : 2 * width] * filtered[:, 2 * width :]
        product = product.astype(jnp.bfloat16)
        owner = lax.broadcasted_iota(jnp.int32, (2 * TAPS, width), 1) // GROUP
        for start in range(0, row_count, TAPS):
            window = product[start : start + 2 * TAPS]
            spread = jnp.concatenate(
                [jnp.where(owner == f, window, jnp.zeros_like(window)) for f in range(filters)], 0
            )
            convolved = jnp.dot(toeplitz_ref[...], spread, preferred_element_type=jnp.float32)
            mixing = skip_ref[...] * window[TAPS:].astype(jnp.float32) + convolved
            queries = filtered[TAPS + start : 2 * TAPS + start, :width]
            out_ref[0, start : start + TAPS] = (queries * mixing).astype(jnp.bfloat16)

    slot = lambda i: (i, 0, 0)
    fixed = lambda i: (0, 0)
    return pl.pallas_call(
        kernel,
        grid=(slots,),
        in_specs=[pl.BlockSpec((1, EDGE, wide), slot)]
        + [pl.BlockSpec((1, part_rows, wide), slot)] * len(parts)
        + [
            pl.BlockSpec((3, wide), fixed),
            pl.BlockSpec((1, width), fixed),
            pl.BlockSpec((TAPS, 2 * TAPS * filters), fixed),
        ],
        out_specs=pl.BlockSpec((1, row_count, width), slot),
        out_shape=jax.ShapeDtypeStruct((slots, row_count, width), jnp.bfloat16),
        scratch_shapes=[pltpu.VMEM((EDGE + row_count, wide), jnp.float32)],
        compiler_params=pltpu.CompilerParams(vmem_limit_bytes=40 << 20),
        cost_estimate=pl.CostEstimate(
            flops=2 * slots * row_count * 2 * TAPS * filters * width,
            bytes_accessed=2 * slots * row_count * 4 * width,
            transcendentals=0,
        ),
        name="gate",
    )(halo, *parts, short_taps, skip_gain, toeplitz)


def out_block(gating, w_out, block, count):
    rows, depth = gating.shape
    columns = w_out.shape[1] // count
    tile = min(columns, 512)
    steps = columns // tile

    def kernel(block_ref, gating_ref, w_ref, out_ref):
        out_ref[...] = jnp.dot(
            gating_ref[...], w_ref[...], preferred_element_type=jnp.float32
        ).astype(jnp.bfloat16)

    return pl.pallas_call(
        kernel,
        grid_spec=pltpu.PrefetchScalarGridSpec(
            num_scalar_prefetch=1,
            grid=(steps,),
            in_specs=[
                pl.BlockSpec((rows, depth), lambda i, b: (0, 0)),
                pl.BlockSpec((depth, tile), lambda i, b: (0, b[0] * steps + i)),
            ],
            out_specs=pl.BlockSpec((rows, tile), lambda i, b: (0, i)),
        ),
        out_shape=jax.ShapeDtypeStruct((rows, columns), jnp.bfloat16),
        compiler_params=pltpu.CompilerParams(vmem_limit_bytes=40 << 20),
        cost_estimate=pl.CostEstimate(
            flops=2 * rows * depth * columns,
            bytes_accessed=2 * (rows * depth + depth * columns + rows * columns),
            transcendentals=0,
        ),
        name="out_block",
    )(block.reshape(1).astype(jnp.int32), gating, w_out)


def toeplitz_of(medium_taps):
    cube_shape = (TAPS, TAPS, 2 * TAPS)
    lagged = (
        lax.broadcasted_iota(jnp.int32, cube_shape, 1)
        + TAPS
        - lax.broadcasted_iota(jnp.int32, cube_shape, 2)
    )
    onehot = (lagged == lax.broadcasted_iota(jnp.int32, cube_shape, 0)).astype(jnp.bfloat16)
    return jnp.einsum("jg,jis->igs", medium_taps.astype(jnp.bfloat16), onehot)


def per_device(tokens, norm_gain, w_in, short_taps, medium_taps, skip_gain, w_out):
    seq, chan = lax.axis_size("seq"), lax.axis_size("chan")
    here, column = lax.axis_index("seq"), lax.axis_index("chan")
    near = seq // 4
    odd, layer = here % 2, here // 2
    half, place = layer // near, layer % near
    row_count = tokens.shape[0]
    depth = norm_gain.shape[0]
    channels = w_in.shape[2]
    mine = channels // near
    pieces = max(1, mine // 128)
    width = mine // pieces
    part_rows = row_count // PARTS

    order = jnp.stack([(place ^ o) * 2 + (odd ^ p) for o in range(near) for p in range(2)])
    order = order.astype(jnp.int32)
    sections = []
    for i in range(pieces):
        held = []
        for o in range(near):
            start = (place ^ o) * mine + i * width
            cut = lax.dynamic_slice_in_dim(w_in, start, width, 2).reshape(w_in.shape[0], 3 * width)
            held.append(cut if o == 0 else swapped(cut, "seq", 2 * o))
        both = []
        for cut in held:
            both += [cut, swapped(cut, "seq", 1)]
        sections.append(both)

    away_rows, own_rows = [], []
    for i in range(PARTS):
        part = tokens[i * part_rows : (i + 1) * part_rows]
        widened = lax.all_to_all(part, "chan", 0, 1, tiled=True).astype(jnp.float32)
        mean_square = jnp.mean(widened * widened, axis=1, keepdims=True)
        normed = (widened * lax.rsqrt(mean_square + EPSILON) * norm_gain).astype(jnp.bfloat16)
        keep = lax.dynamic_slice_in_dim(normed, half * (depth // 2), depth // 2, 1)
        send = lax.dynamic_slice_in_dim(normed, (1 - half) * (depth // 2), depth // 2, 1)
        for rows, kept in ((swapped(send, "seq", 2 * near), away_rows), (keep, own_rows)):
            layers = [rows if o == 0 else swapped(rows, "seq", 2 * o) for o in range(near)]
            rows = lax.all_gather(jnp.stack(layers), "chan", axis=1, tiled=True)
            kept.append(rows.reshape(near * part_rows, depth // 2))

    short = lax.dynamic_slice_in_dim(short_taps, place * mine, mine, 2)
    skip = lax.dynamic_slice_in_dim(skip_gain, place * mine, mine, 0).reshape(1, mine)
    filters = medium_taps.shape[1] // near
    toeplitz = toeplitz_of(lax.dynamic_slice_in_dim(medium_taps, place * filters, filters, 1))
    some = filters // pieces
    far = [(2 * i + 1, 2 * (near + i)) for i in range(near)]
    gates = []
    for i in range(pieces):
        sums = []
        for j in range(PARTS):
            sent = project(order, away_rows[j], sections[i], None)
            sums.append(swapped(sent, "seq", 2 * near))
        sums = [
            project(order, own_rows[j], sections[i], sums[j]).reshape(near, part_rows, 3 * width)
            for j in range(PARTS)
        ]
        edge = sums[-1][:, part_rows - EDGE :]
        edge = jnp.stack([lax.dynamic_index_in_dim(edge, place ^ o, 0, False) for o in range(near)])
        across = swapped(edge, "seq", 1)
        before = jnp.concatenate([lax.ppermute(edge[-1:], "seq", far), across[:-1]], 0)
        halo = jnp.where(odd == 1, across, before)
        halo = jnp.stack([lax.dynamic_index_in_dim(halo, place ^ o, 0, False) for o in range(near)])
        span = slice(i * width, (i + 1) * width)
        gated = gate(
            halo,
            sums,
            short[:, :, span].reshape(3, 3 * width),
            skip[:, span],
            toeplitz[:, i * some : (i + 1) * some].reshape(TAPS, some * 2 * TAPS),
        )
        gates.append([gated[0]] + [swapped(gated[o], "seq", 2 * o) for o in range(1, near)])
    gating = jnp.zeros((row_count, channels), jnp.bfloat16)
    for o in range(near):
        share = jnp.concatenate([piece[o] for piece in gates], 1)
        gating = lax.dynamic_update_slice(gating, share, (0, (place ^ o) * mine))

    total = tokens.astype(jnp.float32)
    for a in reversed(range(chan // 2)):
        target = column ^ (2 * a)
        beside = swapped(out_block(gating, w_out, target ^ 1, chan), "chan", 1)
        summed = out_block(gating, w_out, target, chan).astype(jnp.float32) + beside.astype(jnp.float32)
        if a:
            summed = swapped(summed.astype(jnp.bfloat16), "chan", 2 * a).astype(jnp.float32)
        total += summed
    return total.astype(jnp.bfloat16)


def solution(mesh):
    in_specs = (
        P("seq", "chan"),
        P(),
        P("seq", None, "chan"),
        P(None, None, "chan"),
        P(None, "chan"),
        P("chan"),
        P("chan", None),
    )
    out_specs = P("seq", "chan")
    return jax.shard_map(
        per_device, mesh=mesh, in_specs=in_specs, out_specs=out_specs, check_vma=False
    )
```

time: 1220 us -> 527 us (0.43)
  waiting for transfers between devices: 1070 us -> 241 us
  Pallas kernels: 0 us -> 106 us
  matrix products: 78.4 us -> 3.79 us
  starting transfers between devices: 7.61 us -> 58.4 us
  local copies, waits for them, and re-layouts: 29.3 us -> 63.5 us
  blocking collectives: 0 us -> 17 us
    all_gather x2 -> x4, waiting for transfers between devices: 986 us -> 0.01 us  [per_device(): rows = lax.all_gather(jnp.stack(layers), 'chan', axis=1, tiled=True)]
    ppermute x2 -> x41, waiting for transfers between devices: 6.46 us -> 229 us  [the longest x37 229 us: swapped(): lax.ppermute(value, axis, [(i, i ^ bit) for i in range(lax.axis_size(axis...]
    pallas_call x0 -> x24, Pallas kernels: none -> 106 us  [the longest x16 79.5 us: project(): pl.pallas_call(kernel, grid_spec=pltpu.PrefetchScalarGridSpec(num_scalar_...]
    dot_general x4 -> x1, matrix products: 78.4 us -> 3.79 us  [toeplitz_of(): return jnp.einsum('jg,jis->igs', medium_taps.astype(jnp.bfloat16), onehot)]
    reduce_scatter x1 -> x0, waiting for transfers between devices: 71.8 us -> none  [per_device(): lax.psum_scatter(rounded_out.astype(jnp.bfloat16), 'chan', scatter_dimens...]
    ppermute x2 -> x41, starting transfers between devices: 7.53 us -> 54.7 us  [the longest x37 47.8 us: swapped(): lax.ppermute(value, axis, [(i, i ^ bit) for i in range(lax.axis_size(axis...]
    unnamed x19 -> x93, local copies, waits for them, and re-layouts: 8.96 us -> 37 us
    all_to_all x0 -> x1, blocking collectives: none -> 17 us  [per_device(): widened = lax.all_to_all(part, 'chan', 0, 1, tiled=True).astype(jnp.float32)]
  transfers between devices with their start and end apart: 5 -> 46, of which waited for: 4 -> 22; matrix products, arithmetic and copies ran while one was open for 3% -> 11% of each run, Pallas kernels for 0% -> 19%
where the time goes in v2:
time: 527 us; the launch traced here: 518 us
  waiting for transfers between devices  241 us (46%)
  Pallas kernels  106 us (20%)
  local copies, waits for them, and re-layouts  63.5 us (12%)
  starting transfers between devices  58.4 us (11%)
  blocking collectives  17 us (3%)
  between operations  14.6 us (3%)
  other arithmetic  13.2 us (3%)
    ppermute x37, waiting for transfers between devices, swapped(): lax.ppermute(value, axis, [(i, i ^ bit) for i in range(lax.axis_size(axis...  229 us
    pallas_call x16, Pallas kernels, project(): pl.pallas_call(kernel, grid_spec=pltpu.PrefetchScalarGridSpec(num_scalar_...  79.5 us
    ppermute x37, starting transfers between devices, swapped(): lax.ppermute(value, axis, [(i, i ^ bit) for i in range(lax.axis_size(axis...  47.8 us
    unnamed x93, local copies, waits for them, and re-layouts  37 us
    pallas_call x4, Pallas kernels, out_block(): pl.pallas_call(kernel, grid_spec=pltpu.PrefetchScalarGridSpec(num_scalar_...  19.2 us
    all_to_all x1, blocking collectives, per_device(): widened = lax.all_to_all(part, 'chan', 0, 1, tiled=True).astype(jnp.float32)  17 us
    reshape x8, local copies, waits for them, and re-layouts, per_device(): lax.dynamic_slice_in_dim(w_in, start, width, 2)  14.3 us
    all_to_all x1, waiting for transfers between devices, per_device(): widened = lax.all_to_all(part, 'chan', 0, 1, tiled=True).astype(jnp.float32)  12.6 us
  transfers between devices with their start and end apart: 46, of which 22 were waited for; matrix products, arithmetic and copies ran while one was open for 11% of the time, Pallas kernels for 19%

profile of v2, /device:TPU:4, one launch (start us, length us, event | category | flops | bytes accessed | tf_op | source)
XLA Modules:
  0.0 517.5 jit_solution(14023649578948421485)
XLA Ops:
  9.2 17.0 %all_to_all.26 = bf16[4,64,2048]{2,1,0:T(8,128)(2,1)S(1)} all-to-all(bf16[4,64,2048]{2,1,0:T(8,128)(2,1)S(1)} %bitcast.134), channel_id=1, replica_groups=mesh['seq'=8,'chan'=4] {'chan'}, dimensions={0} | all-to-all | bytes 2097152 | tf_op jit(solution)/shard_map/all_to_all | solution.py:186
  31.6 12.6 %all-to-all-done.1 = bf16[4,64,2048]{2,1,0:T(8,128)(2,1)S(1)} async-done(((bf16[4,64,2048]{2,1,0:T(8,128)(2,1)}), bf16[4,64,2048]{2,1,0:T(8,128)(2,1)S(1)}, u32[]{:S(2)}, u32[]{:S(2)}) %all-to-all-start.1) | async-done | bytes 1048608 | tf_op jit(solution)/shard_map/all_to_all | solution.py:186
  49.4 23.0 %collective-permute-done.10 = bf16[64,4096]{1,0:T(8,128)(2,1)S(1)} collective-permute-done((bf16[64,4096]{1,0:T(8,128)(2,1)S(1)}, bf16[64,4096]{1,0:T(8,128)(2,1)S(1)}, u32[]{:S(2)}, u32[]{:S(2)}) %collective-permute-start.10) | collective-permute-done | bytes 524320 | tf_op jit(solution)/shard_map/ppermute | solution.py:16
  73.1 12.1 %collective-permute-done.11 = bf16[64,4096]{1,0:T(8,128)(2,1)S(1)} collective-permute-done((bf16[64,4096]{1,0:T(8,128)(2,1)S(1)}, bf16[64,4096]{1,0:T(8,128)(2,1)S(1)}, u32[]{:S(2)}, u32[]{:S(2)}) %collective-permute-start.11) | collective-permute-done | bytes 524320 | tf_op jit(solution)/shard_map/ppermute | solution.py:16
  89.9 22.8 %collective-permute-done.4 = bf16[64,4096]{1,0:T(8,128)(2,1)S(1)} collective-permute-done((bf16[64,4096]{1,0:T(8,128)(2,1)S(1)}, bf16[64,4096]{1,0:T(8,128)(2,1)S(1)}, u32[]{:S(2)}, u32[]{:S(2)}) %collective-permute-start.4) | collective-permute-done | bytes 524320 | tf_op jit(solution)/shard_map/ppermute | solution.py:16
  113.4 12.3 %collective-permute-done.5 = bf16[64,4096]{1,0:T(8,128)(2,1)S(1)} collective-permute-done((bf16[64,4096]{1,0:T(8,128)(2,1)S(1)}, bf16[64,4096]{1,0:T(8,128)(2,1)S(1)}, u32[]{:S(2)}, u32[]{:S(2)}) %collective-permute-start.5) | collective-permute-done | bytes 524320 | tf_op jit(solution)/shard_map/ppermute | solution.py:16
  128.4 11.2 %collective-permute-done = bf16[64,4096]{1,0:T(8,128)(2,1)S(1)} collective-permute-done((bf16[64,4096]{1,0:T(8,128)(2,1)S(1)}, bf16[64,4096]{1,0:T(8,128)(2,1)S(1)}, u32[]{:S(2)}, u32[]{:S(2)}) %collective-permute-start) | collective-permute-done | bytes 524320 | tf_op jit(solution)/shard_map/ppermute | solution.py:16
  142.5 10.3 %collective-permute-done.9 = bf16[64,4096]{1,0:T(8,128)(2,1)S(1)} collective-permute-done((bf16[64,4096]{1,0:T(8,128)(2,1)S(1)}, bf16[64,4096]{1,0:T(8,128)(2,1)S(1)}, u32[]{:S(2)}, u32[]{:S(2)}) %collective-permute-start.9) | collective-permute-done | bytes 524320 | tf_op jit(solution)/shard_map/ppermute | solution.py:16
  154.0 5.0 constant_dynamic-slice_fusion.29
  190.2 9.9 %collective-permute-done.14.refs_2_ = bf16[1024,384]{1,0:T(8,128)(2,1)} collective-permute-done((bf16[1024,384]{1,0:T(8,128)(2,1)}, bf16[1024,384]{1,0:T(8,128)(2,1)}, u32[]{:S(2)}, u32[]{:S(2)}) %collective-permute-start.14) | collective-permute-done | bytes 786464 | tf_op jit(solution)/shard_map/ppermute | solution.py:16
  217.7 12.5 %collective-permute-done.28.refs_2_ = bf16[1024,384]{1,0:T(8,128)(2,1)} collective-permute-done((bf16[1024,384]{1,0:T(8,128)(2,1)}, bf16[1024,384]{1,0:T(8,128)(2,1)}, u32[]{:S(2)}, u32[]{:S(2)}) %collective-permute-start.28) | collective-permute-done | bytes 786464 | tf_op jit(solution)/shard_map/ppermute | solution.py:16
  235.6 5.1 project.18
  244.0 5.1 project.16
  258.4 5.4 %project.22 = bf16[512,384]{1,0:T(8,128)(2,1)} custom-call(s32[4]{0:T(128)S(1)} %pad_add_fusion.order_ref, bf16[512,4096]{1,0:T(8,128)(2,1)S(1)} %bitcast.101, bf16[1024,384]{1,0:T(8,128)(2,1)S(1)} %copy.33.refs_0_, bf16[1024,384]{1,0:T(8,128)(2,1)} %collective-permute-done.13.refs_1_, bf16[1024,384]{1,0:T(8,128)(2,1)} %collective-permute-done.14.refs_2_, ...), custom_call_target="tpu_custom_call" | custom-call | flops 1610612736 | bytes 7733248 | tf_op jit(solution)/shard_map/project/pallas_call | solution.py:36
  264.1 5.7 %collective-permute-done.22.refs_3_ = bf16[1024,384]{1,0:T(8,128)(2,1)} collective-permute-done((bf16[1024,384]{1,0:T(8,128)(2,1)}, bf16[1024,384]{1,0:T(8,128)(2,1)}, u32[]{:S(2)}, u32[]{:S(2)}) %collective-permute-start.22) | collective-permute-done | bytes 786464 | tf_op jit(solution)/shard_map/ppermute | solution.py:16
  273.3 5.4 %project.26 = bf16[512,384]{1,0:T(8,128)(2,1)} custom-call(s32[4]{0:T(128)S(1)} %pad_add_fusion.order_ref, bf16[512,4096]{1,0:T(8,128)(2,1)S(1)} %bitcast.102, bf16[1024,384]{1,0:T(8,128)(2,1)S(1)} %copy.41.refs_0_, bf16[1024,384]{1,0:T(8,128)(2,1)} %collective-permute-done.20.refs_1_, bf16[1024,384]{1,0:T(8,128)(2,1)} %collective-permute-done.21.refs_2_, ...), custom_call_target="tpu_custom_call" | custom-call | flops 1610612736 | bytes 7733248 | tf_op jit(solution)/shard_map/project/pallas_call | solution.py:36
  278.6 4.9 project.24
  290.1 9.4 %collective-permute-done.29.refs_3_ = bf16[1024,384]{1,0:T(8,128)(2,1)} collective-permute-done((bf16[1024,384]{1,0:T(8,128)(2,1)}, bf16[1024,384]{1,0:T(8,128)(2,1)}, u32[]{:S(2)}, u32[]{:S(2)}) %collective-permute-start.29) | collective-permute-done | bytes 786464 | tf_op jit(solution)/shard_map/ppermute | solution.py:16
  303.1 5.4 %project.28 = bf16[512,384]{1,0:T(8,128)(2,1)} custom-call(s32[4]{0:T(128)S(1)} %pad_add_fusion.order_ref, bf16[512,4096]{1,0:T(8,128)(2,1)S(1)} %bitcast.111, bf16[1024,384]{1,0:T(8,128)(2,1)S(1)} %copy.49.refs_0_, bf16[1024,384]{1,0:T(8,128)(2,1)} %collective-permute-done.27.refs_1_, bf16[1024,384]{1,0:T(8,128)(2,1)} %collective-permute-done.28.refs_2_, ...), custom_call_target="tpu_custom_call" | custom-call | flops 1610612736 | bytes 7733248 | tf_op jit(solution)/shard_map/project/pallas_call | solution.py:36
  308.5 5.4 %project.30 = bf16[512,384]{1,0:T(8,128)(2,1)} custom-call(s32[4]{0:T(128)S(1)} %pad_add_fusion.order_ref, bf16[512,4096]{1,0:T(8,128)(2,1)S(1)} %bitcast.103, bf16[1024,384]{1,0:T(8,128)(2,1)S(1)} %copy.49.refs_0_, bf16[1024,384]{1,0:T(8,128)(2,1)} %collective-permute-done.27.refs_1_, bf16[1024,384]{1,0:T(8,128)(2,1)} %collective-permute-done.28.refs_2_, ...), custom_call_target="tpu_custom_call" | custom-call | flops 1610612736 | bytes 7733248 | tf_op jit(solution)/shard_map/project/pallas_call | solution.py:36
  332.5 28.3 %collective-permute-done.30.refs_4_ = bf16[512,384]{1,0:T(8,128)(2,1)} collective-permute-done((bf16[512,384]{1,0:T(8,128)(2,1)}, bf16[512,384]{1,0:T(8,128)(2,1)}, u32[]{:S(2)}, u32[]{:S(2)}) %collective-permute-start.30) | collective-permute-done | bytes 393248 | tf_op jit(solution)/shard_map/ppermute | solution.py:16
  360.9 4.8 project.29
  366.4 11.2 %collective-permute-done.23.refs_4_ = bf16[512,384]{1,0:T(8,128)(2,1)S(1)} collective-permute-done((bf16[512,384]{1,0:T(8,128)(2,1)S(1)}, bf16[512,384]{1,0:T(8,128)(2,1)S(1)}, u32[]{:S(2)}, u32[]{:S(2)}) %collective-permute-start.23) | collective-permute-done | bytes 393248 | tf_op jit(solution)/shard_map/ppermute | solution.py:16
  379.6 4.7 project.25
  396.8 5.1 project.23
  402.0 4.9 project.27
  408.9 4.8 project.31
  442.2 4.8 out_block.5
  447.0 4.8 out_block.7
  452.4 4.8 out_block.4
  460.3 4.9 out_block.6
  465.2 42.0 %collective-permute-done.39 = bf16[512,2048]{1,0:T(8,128)(2,1)S(1)} collective-permute-done((bf16[512,2048]{1,0:T(8,128)(2,1)S(1)}, bf16[512,2048]{1,0:T(8,128)(2,1)S(1)}, u32[]{:S(2)}, u32[]{:S(2)}) %collective-permute-start.39) | collective-permute-done | bytes 2097184 | tf_op jit(solution)/shard_map/ppermute | solution.py:16
  (248 shorter events, 177.3 us)
Async XLA Ops:
  26.3 18.0 %all-to-all-start.1 = ((bf16[4,64,2048]{2,1,0:T(8,128)(2,1)}), bf16[4,64,2048]{2,1,0:T(8,128)(2,1)S(1)}, u32[]{:S(2)}, u32[]{:S(2)}) async-start(bf16[4,64,2048]{2,1,0:T(8,128)(2,1)} %bitcast.16), calls=%async_computation.1 | async-start | bytes 2097152 | tf_op jit(solution)/shard_map/all_to_all | solution.py:186
  29.8 202.4 %all-gather.11.cloned.1.call-start = ((), (), s32[]{:S(2)}) async-start(), calls=%async_computation.5 | async-start | bytes 5242880 | tf_op jit(solution)/shard_map/all_gather | solution.py:193
  46.7 25.7 %collective-permute-start.10 = (bf16[64,4096]{1,0:T(8,128)(2,1)S(1)}, bf16[64,4096]{1,0:T(8,128)(2,1)S(1)}, u32[]{:S(2)}, u32[]{:S(2)}) collective-permute-start(bf16[64,4096]{1,0:T(8,128)(2,1)S(1)} %get-tuple-element.19), channel_id=1, source_target_pairs={{0,16},{4,20},{8,24},{12,28},{16,0},{20,4},{24,8},{28,12},{1,17},{... | collective-permute-start | bytes 1572872 | tf_op jit(solution)/shard_map/ppermute | solution.py:16
  86.3 154.4 %all-gather.7.cloned.1.call-start = ((), (), s32[]{:S(2)}) async-start(), calls=%async_computation.3 | async-start | bytes 5242880 | tf_op jit(solution)/shard_map/all_gather | solution.py:193
  86.4 26.2 %collective-permute-start.4 = (bf16[64,4096]{1,0:T(8,128)(2,1)S(1)}, bf16[64,4096]{1,0:T(8,128)(2,1)S(1)}, u32[]{:S(2)}, u32[]{:S(2)}) collective-permute-start(bf16[64,4096]{1,0:T(8,128)(2,1)S(1)} %get-tuple-element.21), channel_id=1, source_target_pairs={{0,16},{4,20},{8,24},{12,28},{16,0},{20,4},{24,8},{28,12},{1,17},{... | collective-permute-start | bytes 1572872 | tf_op jit(solution)/shard_map/ppermute | solution.py:16
  126.7 187.9 %all-gather.5.cloned.1.call-start = ((), (), s32[]{:S(2)}) async-start(), calls=%async_computation.2 | async-start | bytes 5242880 | tf_op jit(solution)/shard_map/all_gather | solution.py:193
  140.7 246.3 %all-gather.9.cloned.1.call-start = ((), (), s32[]{:S(2)}) async-start(), calls=%async_computation.4 | async-start | bytes 5242880 | tf_op jit(solution)/shard_map/all_gather | solution.py:193
  162.5 23.4 %collective-permute-start.2 = (bf16[1024,384]{1,0:T(8,128)(2,1)}, bf16[1024,384]{1,0:T(8,128)(2,1)}, u32[]{:S(2)}, u32[]{:S(2)}) collective-permute-start(bf16[1024,384]{1,0:T(8,128)(2,1)} %copy.22), channel_id=1, source_target_pairs={{0,8},{4,12},{8,0},{12,4},{16,24},{20,28},{24,16},{28,20},{1,9},{5... | collective-permute-start | bytes 2359304 | tf_op jit(solution)/shard_map/ppermute | solution.py:16
  164.9 21.2 %collective-permute-start.1 = (bf16[1024,384]{1,0:T(8,128)(2,1)S(1)}, bf16[1024,384]{1,0:T(8,128)(2,1)S(1)}, u32[]{:S(2)}, u32[]{:S(2)}) collective-permute-start(bf16[1024,384]{1,0:T(8,128)(2,1)S(1)} %copy.24.refs_0_), channel_id=1, source_target_pairs={{0,4},{4,0},{8,12},{12,8},{16,20},{20,16},{24,28},{28,24},{1,5},{5... | collective-permute-start | bytes 2359304 | tf_op jit(solution)/shard_map/ppermute | solution.py:16
  170.0 30.1 %collective-permute-start.14 = (bf16[1024,384]{1,0:T(8,128)(2,1)}, bf16[1024,384]{1,0:T(8,128)(2,1)}, u32[]{:S(2)}, u32[]{:S(2)}) collective-permute-start(bf16[1024,384]{1,0:T(8,128)(2,1)} %copy.31), channel_id=1, source_target_pairs={{0,8},{4,12},{8,0},{12,4},{16,24},{20,28},{24,16},{28,20},{1,9},{5... | collective-permute-start | bytes 2359304 | tf_op jit(solution)/shard_map/ppermute | solution.py:16
  173.1 42.5 %collective-permute-start.13 = (bf16[1024,384]{1,0:T(8,128)(2,1)S(1)}, bf16[1024,384]{1,0:T(8,128)(2,1)}, u32[]{:S(2)}, u32[]{:S(2)}) collective-permute-start(bf16[1024,384]{1,0:T(8,128)(2,1)S(1)} %copy.33.refs_0_), channel_id=1, source_target_pairs={{0,4},{4,0},{8,12},{12,8},{16,20},{20,16},{24,28},{28,24},{1,5},{5... | collective-permute-start | bytes 2359304 | tf_op jit(solution)/shard_map/ppermute | solution.py:16
  179.4 38.0 %collective-permute-start.21 = (bf16[1024,384]{1,0:T(8,128)(2,1)}, bf16[1024,384]{1,0:T(8,128)(2,1)}, u32[]{:S(2)}, u32[]{:S(2)}) collective-permute-start(bf16[1024,384]{1,0:T(8,128)(2,1)} %copy.39), channel_id=1, source_target_pairs={{0,8},{4,12},{8,0},{12,4},{16,24},{20,28},{24,16},{28,20},{1,9},{5... | collective-permute-start | bytes 2359304 | tf_op jit(solution)/shard_map/ppermute | solution.py:16
  185.8 44.4 %collective-permute-start.28 = (bf16[1024,384]{1,0:T(8,128)(2,1)}, bf16[1024,384]{1,0:T(8,128)(2,1)}, u32[]{:S(2)}, u32[]{:S(2)}) collective-permute-start(bf16[1024,384]{1,0:T(8,128)(2,1)} %copy.47), channel_id=1, source_target_pairs={{0,8},{4,12},{8,0},{12,4},{16,24},{20,28},{24,16},{28,20},{1,9},{5... | collective-permute-start | bytes 2359304 | tf_op jit(solution)/shard_map/ppermute | solution.py:16
  186.0 44.7 %collective-permute-start.3 = (bf16[1024,384]{1,0:T(8,128)(2,1)}, bf16[1024,384]{1,0:T(8,128)(2,1)}, u32[]{:S(2)}, u32[]{:S(2)}) collective-permute-start(bf16[1024,384]{1,0:T(8,128)(2,1)} %collective-permute-done.2.refs_2_), channel_id=1, source_target_pairs={{0,4},{4,0},{8,12},{12,8},{16,20},{20,16},{24,28},{28,24},{1,5},{5... | collective-permute-start | bytes 2359304 | tf_op jit(solution)/shard_map/ppermute | solution.py:16
  200.1 49.0 %collective-permute-start.15 = (bf16[1024,384]{1,0:T(8,128)(2,1)}, bf16[1024,384]{1,0:T(8,128)(2,1)}, u32[]{:S(2)}, u32[]{:S(2)}) collective-permute-start(bf16[1024,384]{1,0:T(8,128)(2,1)} %collective-permute-done.14.refs_2_), channel_id=1, source_target_pairs={{0,4},{4,0},{8,12},{12,8},{16,20},{20,16},{24,28},{28,24},{1,5},{5... | collective-permute-start | bytes 2359304 | tf_op jit(solution)/shard_map/ppermute | solution.py:16
  215.6 48.1 %collective-permute-start.20 = (bf16[1024,384]{1,0:T(8,128)(2,1)S(1)}, bf16[1024,384]{1,0:T(8,128)(2,1)}, u32[]{:S(2)}, u32[]{:S(2)}) collective-permute-start(bf16[1024,384]{1,0:T(8,128)(2,1)S(1)} %copy.41.refs_0_), channel_id=1, source_target_pairs={{0,4},{4,0},{8,12},{12,8},{16,20},{20,16},{24,28},{28,24},{1,5},{5... | collective-permute-start | bytes 2359304 | tf_op jit(solution)/shard_map/ppermute | solution.py:16
  217.3 52.4 %collective-permute-start.22 = (bf16[1024,384]{1,0:T(8,128)(2,1)}, bf16[1024,384]{1,0:T(8,128)(2,1)}, u32[]{:S(2)}, u32[]{:S(2)}) collective-permute-start(bf16[1024,384]{1,0:T(8,128)(2,1)} %collective-permute-done.21.refs_2_), channel_id=1, source_target_pairs={{0,4},{4,0},{8,12},{12,8},{16,20},{20,16},{24,28},{28,24},{1,5},{5... | collective-permute-start | bytes 2359304 | tf_op jit(solution)/shard_map/ppermute | solution.py:16
  230.2 56.4 %collective-permute-start.27 = (bf16[1024,384]{1,0:T(8,128)(2,1)S(1)}, bf16[1024,384]{1,0:T(8,128)(2,1)}, u32[]{:S(2)}, u32[]{:S(2)}) collective-permute-start(bf16[1024,384]{1,0:T(8,128)(2,1)S(1)} %copy.49.refs_0_), channel_id=1, source_target_pairs={{0,4},{4,0},{8,12},{12,8},{16,20},{20,16},{24,28},{28,24},{1,5},{5... | collective-permute-start | bytes 2359304 | tf_op jit(solution)/shard_map/ppermute | solution.py:16
  230.7 68.9 %collective-permute-start.29 = (bf16[1024,384]{1,0:T(8,128)(2,1)}, bf16[1024,384]{1,0:T(8,128)(2,1)}, u32[]{:S(2)}, u32[]{:S(2)}) collective-permute-start(bf16[1024,384]{1,0:T(8,128)(2,1)} %collective-permute-done.28.refs_2_), channel_id=1, source_target_pairs={{0,4},{4,0},{8,12},{12,8},{16,20},{20,16},{24,28},{28,24},{1,5},{5... | collective-permute-start | bytes 2359304 | tf_op jit(solution)/shard_map/ppermute | solution.py:16
  249.2 135.9 %collective-permute-start.12 = (bf16[512,384]{1,0:T(8,128)(2,1)}, bf16[512,384]{1,0:T(8,128)(2,1)}, u32[]{:S(2)}, u32[]{:S(2)}) collective-permute-start(bf16[512,384]{1,0:T(8,128)(2,1)} %project.18), channel_id=1, source_target_pairs={{0,16},{4,20},{8,24},{12,28},{16,0},{20,4},{24,8},{28,12},{1,17},{... | collective-permute-start | bytes 1179656 | tf_op jit(solution)/shard_map/ppermute | solution.py:16
  263.8 50.1 %collective-permute-start.16 = (bf16[512,384]{1,0:T(8,128)(2,1)S(1)}, bf16[512,384]{1,0:T(8,128)(2,1)S(1)}, u32[]{:S(2)}, u32[]{:S(2)}) collective-permute-start(bf16[512,384]{1,0:T(8,128)(2,1)S(1)} %project.20), channel_id=1, source_target_pairs={{0,16},{4,20},{8,24},{12,28},{16,0},{20,4},{24,8},{28,12},{1,17},{... | collective-permute-start | bytes 1179656 | tf_op jit(solution)/shard_map/ppermute | solution.py:16
  269.8 57.4 %collective-permute-start.6 = (bf16[512,384]{1,0:T(8,128)(2,1)}, bf16[512,384]{1,0:T(8,128)(2,1)}, u32[]{:S(2)}, u32[]{:S(2)}) collective-permute-start(bf16[512,384]{1,0:T(8,128)(2,1)} %project.16), channel_id=1, source_target_pairs={{0,16},{4,20},{8,24},{12,28},{16,0},{20,4},{24,8},{28,12},{1,17},{... | collective-permute-start | bytes 1179656 | tf_op jit(solution)/shard_map/ppermute | solution.py:16
  286.6 108.6 %collective-permute-start.19 = (bf16[512,384]{1,0:T(8,128)(2,1)}, bf16[512,384]{1,0:T(8,128)(2,1)}, u32[]{:S(2)}, u32[]{:S(2)}) collective-permute-start(bf16[512,384]{1,0:T(8,128)(2,1)} %project.22), channel_id=1, source_target_pairs={{0,16},{4,20},{8,24},{12,28},{16,0},{20,4},{24,8},{28,12},{1,17},{... | collective-permute-start | bytes 1179656 | tf_op jit(solution)/shard_map/ppermute | solution.py:16
  299.6 102.3 %collective-permute-start.26 = (bf16[512,384]{1,0:T(8,128)(2,1)}, bf16[512,384]{1,0:T(8,128)(2,1)}, u32[]{:S(2)}, u32[]{:S(2)}) collective-permute-start(bf16[512,384]{1,0:T(8,128)(2,1)} %project.26), channel_id=1, source_target_pairs={{0,16},{4,20},{8,24},{12,28},{16,0},{20,4},{24,8},{28,12},{1,17},{... | collective-permute-start | bytes 1179656 | tf_op jit(solution)/shard_map/ppermute | solution.py:16
  314.6 46.2 %collective-permute-start.30 = (bf16[512,384]{1,0:T(8,128)(2,1)}, bf16[512,384]{1,0:T(8,128)(2,1)}, u32[]{:S(2)}, u32[]{:S(2)}) collective-permute-start(bf16[512,384]{1,0:T(8,128)(2,1)} %project.28), channel_id=1, source_target_pairs={{0,16},{4,20},{8,24},{12,28},{16,0},{20,4},{24,8},{28,12},{1,17},{... | collective-permute-start | bytes 1179656 | tf_op jit(solution)/shard_map/ppermute | solution.py:16
  327.1 50.5 %collective-permute-start.23 = (bf16[512,384]{1,0:T(8,128)(2,1)S(1)}, bf16[512,384]{1,0:T(8,128)(2,1)S(1)}, u32[]{:S(2)}, u32[]{:S(2)}) collective-permute-start(bf16[512,384]{1,0:T(8,128)(2,1)S(1)} %copy-done.28), channel_id=1, source_target_pairs={{0,16},{4,20},{8,24},{12,28},{16,0},{20,4},{24,8},{28,12},{1,17},{... | collective-permute-start | bytes 1179656 | tf_op jit(solution)/shard_map/ppermute | solution.py:16
  360.8 46.0 %collective-permute-start.33 = (bf16[512,384]{1,0:T(8,128)(2,1)}, bf16[512,384]{1,0:T(8,128)(2,1)}, u32[]{:S(2)}, u32[]{:S(2)}) collective-permute-start(bf16[512,384]{1,0:T(8,128)(2,1)} %project.30), channel_id=1, source_target_pairs={{0,16},{4,20},{8,24},{12,28},{16,0},{20,4},{24,8},{28,12},{1,17},{... | collective-permute-start | bytes 1179656 | tf_op jit(solution)/shard_map/ppermute | solution.py:16
  377.6 37.8 %collective-permute-start.18 = (bf16[1,144,384]{2,1,0:T(8,128)(2,1)S(1)}, bf16[1,144,384]{2,1,0:T(8,128)(2,1)}, u32[]{:S(2)}, u32[]{:S(2)}) collective-permute-start(bf16[1,144,384]{2,1,0:T(8,128)(2,1)S(1)} %get-tuple-element.38), channel_id=1, source_target_pairs={{4,16},{12,24},{5,17},{13,25},{6,18},{14,26},{7,19},{15,27}} | collective-permute-start | bytes 331784 | tf_op jit(solution)/shard_map/ppermute | solution.py:215
  385.1 32.4 %collective-permute-start.8 = (bf16[1,144,384]{2,1,0:T(8,128)(2,1)S(1)}, bf16[1,144,384]{2,1,0:T(8,128)(2,1)}, u32[]{:S(2)}, u32[]{:S(2)}) collective-permute-start(bf16[1,144,384]{2,1,0:T(8,128)(2,1)S(1)} %get-tuple-element.34), channel_id=1, source_target_pairs={{4,16},{12,24},{5,17},{13,25},{6,18},{14,26},{7,19},{15,27}} | collective-permute-start | bytes 331784 | tf_op jit(solution)/shard_map/ppermute | solution.py:215
  395.2 31.2 %collective-permute-start.32 = (bf16[1,144,384]{2,1,0:T(8,128)(2,1)S(1)}, bf16[1,144,384]{2,1,0:T(8,128)(2,1)S(1)}, u32[]{:S(2)}, u32[]{:S(2)}) collective-permute-start(bf16[1,144,384]{2,1,0:T(8,128)(2,1)S(1)} %get-tuple-element.46), channel_id=1, source_target_pairs={{4,16},{12,24},{5,17},{13,25},{6,18},{14,26},{7,19},{15,27}} | collective-permute-start | bytes 331784 | tf_op jit(solution)/shard_map/ppermute | solution.py:215
  451.8 13.4 %collective-permute-start.40 = (bf16[512,2048]{1,0:T(8,128)(2,1)S(1)}, bf16[512,2048]{1,0:T(8,128)(2,1)S(1)}, u32[]{:S(2)}, u32[]{:S(2)}) collective-permute-start(bf16[512,2048]{1,0:T(8,128)(2,1)S(1)} %out_block.7), channel_id=1, source_target_pairs={{0,1},{1,0},{2,3},{3,2},{4,5},{5,4},{6,7},{7,6},{8,9},{9,8},{10,11... | collective-permute-start | bytes 6291464 | tf_op jit(solution)/shard_map/ppermute | solution.py:16
  459.6 47.6 %collective-permute-start.39 = (bf16[512,2048]{1,0:T(8,128)(2,1)S(1)}, bf16[512,2048]{1,0:T(8,128)(2,1)S(1)}, u32[]{:S(2)}, u32[]{:S(2)}) collective-permute-start(bf16[512,2048]{1,0:T(8,128)(2,1)S(1)} %add_convert_fusion.1), channel_id=1, source_target_pairs={{0,2},{1,3},{2,0},{3,1},{4,6},{5,7},{6,4},{7,5},{8,10},{9,11},{10,... | collective-permute-start | bytes 6291464 | tf_op jit(solution)/shard_map/ppermute | solution.py:16
  (52 other events, 596.9 us)
Sparse Core Ops, SparseCore 0:
  86.4 35.7 all-gather.10
  126.8 35.5 all-gather.6
  164.0 34.4 all-gather.4
  199.9 34.4 all-gather.8

commit v3 on v2

--- a/solution.py
+++ b/solution.py
@@ -16,42 +16,49 @@
     return lax.ppermute(value, axis, [(i, i ^ bit) for i in range(lax.axis_size(axis))])
 
 
-def project(order, rows, sections, addend):
-    count, depth = rows.shape
+def project(order, places, rows, sections, addend, near):
+    ranks = len(rows)
+    depth = rows[0].shape[1]
     step, width = sections[0].shape
+    each = rows[0].shape[0] // near
+    span = ranks * each
+    count = near * span
     tile = min(count, 256)
 
-    def kernel(order_ref, rows_ref, *refs):
-        total = jnp.zeros((tile, width), jnp.float32)
-        for i in range(len(sections)):
-            place = pl.ds(pl.multiple_of(order_ref[i] * step, step), step)
-            total += jnp.dot(rows_ref[:, place], refs[i][...], preferred_element_type=jnp.float32)
-        if addend is not None:
-            total += refs[len(sections)][...].astype(jnp.float32)
-        refs[-1][...] = total.astype(jnp.bfloat16)
-
-    whole = pl.BlockSpec((step, width), lambda i, _: (0, 0))
-    piece = pl.BlockSpec((tile, width), lambda i, _: (i, 0))
+    def kernel(order_ref, places_ref, *refs):
+        gathered, out_ref = refs[-1], refs[-2]
+        for i in range(ranks):
+            place = pl.multiple_of(places_ref[i] * each, each)
+            for o in range(near):
+                gathered[pl.ds(o * span + place, each)] = refs[i][o * each : (o + 1) * each]
+        section_refs = refs[ranks : ranks + len(sections)]
+        for start in range(0, count, tile):
+            here = slice(start, start + tile)
+            total = jnp.zeros((tile, width), jnp.float32)
+            for i, ref in enumerate(section_refs):
+                place = pl.ds(pl.multiple_of(order_ref[i] * step, step), step)
+                total += jnp.dot(gathered[here, place], ref[...], preferred_element_type=jnp.float32)
+            if addend is not None:
+                total += refs[-3][here].astype(jnp.float32)
+            out_ref[here] = total.astype(jnp.bfloat16)
+
     extra = [] if addend is None else [addend]
+    smem = pl.BlockSpec(memory_space=pltpu.SMEM)
+    vmem = pl.BlockSpec(memory_space=pltpu.VMEM)
     return pl.pallas_call(
         kernel,
-        grid_spec=pltpu.PrefetchScalarGridSpec(
-            num_scalar_prefetch=1,
-            grid=(count // tile,),
-            in_specs=[pl.BlockSpec((tile, depth), lambda i, _: (i, 0))]
-            + [whole] * len(sections)
-            + [piece] * len(extra),
-            out_specs=piece,
-        ),
+        in_specs=[smem, smem] + [vmem] * (ranks + len(sections) + len(extra)),
+        out_specs=vmem,
         out_shape=jax.ShapeDtypeStruct((count, width), jnp.bfloat16),
-        compiler_params=pltpu.CompilerParams(vmem_limit_bytes=40 << 20),
+        scratch_shapes=[pltpu.VMEM((count, depth), jnp.bfloat16)],
+        compiler_params=pltpu.CompilerParams(vmem_limit_bytes=32 << 20),
         cost_estimate=pl.CostEstimate(
             flops=2 * count * depth * width,
             bytes_accessed=2 * (count * depth + depth * width + count * width),
             transcendentals=0,
         ),
         name="project",
-    )(order, rows, *sections, *extra)
+    )(order, places, *rows, *sections, *extra)
 
 
 def gate(halo, parts, short_taps, skip_gain, toeplitz):
@@ -166,32 +173,146 @@
     width = mine // pieces
     part_rows = row_count // PARTS
 
+    ranks = chan
+    each = part_rows // ranks
     order = jnp.stack([(place ^ o) * 2 + (odd ^ p) for o in range(near) for p in range(2)])
     order = order.astype(jnp.int32)
-    sections = []
+    places = jnp.stack([column ^ i for i in range(ranks)]).astype(jnp.int32)
+
+    def cut(i, o):
+        start = (place ^ o) * mine + i * width
+        return lax.dynamic_slice_in_dim(w_in, start, width, 2).reshape(w_in.shape[0], 3 * width)
+
+    def share_out(part):
+        parts = [lax.dynamic_slice_in_dim(part, (column ^ i) * each, each, 0) for i in range(ranks)]
+        return [rows if i == 0 else swapped(rows, "chan", i) for i, rows in enumerate(parts)]
+
+    def normed_halves(pieces):
+        widened = [piece.astype(jnp.float32) for piece in pieces]
+        square = sum(jnp.sum(piece * piece, axis=1, keepdims=True) for piece in widened)
+        scale = lax.rsqrt(square / depth + EPSILON)
+        gains = norm_gain.reshape(ranks, 1, depth // ranks)
+        normed = jnp.stack(
+            [
+                (piece * scale * lax.dynamic_index_in_dim(gains, column ^ i, 0, False)).astype(jnp.bfloat16)
+                for i, piece in enumerate(widened)
+            ]
+        )
+
+        def of_half(which):
+            chosen = [
+                lax.dynamic_index_in_dim(normed, column ^ (which * (ranks // 2) + i), 0, False)
+                for i in range(ranks // 2)
+            ]
+            return jnp.concatenate(chosen, 1)
+
+        return of_half(half), of_half(1 - half)
+
+    def near_rows(rows):
+        return jnp.concatenate(
+            [rows if o == 0 else swapped(rows, "seq", 2 * o) for o in range(near)], 0
+        )
+
+    def chan_rows(rows):
+        across = [rows if a == 0 else swapped(rows, "chan", 2 * a) for a in range(ranks // 2)]
+        return [moved for value in across for moved in (value, swapped(value, "chan", 1))]
+
+    def near_cuts(cuts):
+        return [value if o == 0 else swapped(value, "seq", 2 * o) for o, value in enumerate(cuts)]
+
+    hold = lax.optimization_barrier
+    cuts = [[cut(i, o) for o in range(near)] for i in range(pieces)]
+    parts = [tokens[i * part_rows : (i + 1) * part_rows] for i in range(PARTS)]
+
+    def paired(i):
+        return swapped(cuts[i][0], "seq", 1)
+
+    def paired_near(i):
+        return [swapped(value, "seq", 1) for value in nears[i][1:]]
+
+    nears, own_pair, near_pair = [None] * pieces, [None] * pieces, [None] * pieces
+    away, kept = [None] * PARTS, [None] * PARTS
+    away_rows, own_rows = [None] * PARTS, [None] * PARTS
+    sums = [[None] * PARTS for _ in range(pieces)]
+    moved = [[None] * PARTS for _ in range(pieces)]
+
+    def sections(i):
+        both = []
+        for o in range(near):
+            both += [nears[i][o], own_pair[i] if o == 0 else near_pair[i][o - 1]]
+        return both
+
+    def send_partial(i, j):
+        sent = project(order, places, away_rows[j], sections(i), None, near)
+        moved[i][j] = swapped(sent, "seq", 2 * near)
+
+    def add_partial(i, j):
+        sums[i][j] = project(order, places, own_rows[j], sections(i), moved[i][j], near)
+
+    last = pieces - 1
+    two = min(1, last)
+    shared = share_out(parts[0])
+    own_pair[0] = paired(0)
+    nears[0] = near_cuts(cuts[0])
+    shared, own_pair, nears, cuts, parts = hold((shared, own_pair, nears, cuts, parts))
+    kept[0], send = normed_halves(shared)
+    away[0] = swapped(send, "seq", 2 * near)
+    shared = share_out(parts[1])
+    near_pair[0] = paired_near(0)
+    kept, away, shared, near_pair, cuts = hold((kept, away, shared, near_pair, cuts))
+    kept[1], send = normed_halves(shared)
+    away[1] = swapped(send, "seq", 2 * near)
+    away[0] = near_rows(away[0])
+    if last > 0:
+        own_pair[1] = paired(1)
+        nears[1] = near_cuts(cuts[1])
+    kept, away, own_pair, nears, cuts = hold((kept, away, own_pair, nears, cuts))
+    away_rows[0] = chan_rows(away[0])
+    away[1] = near_rows(away[1])
+    if last > 0:
+        near_pair[1] = paired_near(1)
+    if last > 1:
+        nears[2] = near_cuts(cuts[2])
+    kept, away, away_rows, near_pair, nears, cuts = hold(
+        (kept, away, away_rows, near_pair, nears, cuts)
+    )
+    send_partial(0, 0)
+    away_rows[1] = chan_rows(away[1])
+    kept[0] = near_rows(kept[0])
+    if last > 1:
+        own_pair[2] = paired(2)
+    if last > 2:
+        nears[3] = near_cuts(cuts[3])
+    moved, away_rows, kept, own_pair, nears, cuts = hold(
+        (moved, away_rows, kept, own_pair, nears, cuts)
+    )
+    send_partial(0, 1)
+    own_rows[0] = chan_rows(kept[0])
+    kept[1] = near_rows(kept[1])
+    if last > 0:
+        send_partial(1, 0)
+    if last > 1:
+        near_pair[2] = paired_near(2)
+    moved, own_rows, kept, near_pair, cuts = hold((moved, own_rows, kept, near_pair, cuts))
+    own_rows[1] = chan_rows(kept[1])
+    if last > 0:
+        send_partial(1, 1)
+    if last > 1:
+        send_partial(2, 0)
+    if last > 2:
+        own_pair[3] = paired(3)
+    moved, own_rows, own_pair, nears = hold((moved, own_rows, own_pair, nears))
+    if last > 1:
+        send_partial(2, 1)
+    if last > 2:
+        near_pair[3] = paired_near(3)
+    moved, near_pair = hold((moved, near_pair))
+    if last > 2:
+        send_partial(3, 0)
+        send_partial(3, 1)
     for i in range(pieces):
-        held = []
-        for o in range(near):
-            start = (place ^ o) * mine + i * width
-            cut = lax.dynamic_slice_in_dim(w_in, start, width, 2).reshape(w_in.shape[0], 3 * width)
-            held.append(cut if o == 0 else swapped(cut, "seq", 2 * o))
-        both = []
-        for cut in held:
-            both += [cut, swapped(cut, "seq", 1)]
-        sections.append(both)
-
-    away_rows, own_rows = [], []
-    for i in range(PARTS):
-        part = tokens[i * part_rows : (i + 1) * part_rows]
-        widened = lax.all_to_all(part, "chan", 0, 1, tiled=True).astype(jnp.float32)
-        mean_square = jnp.mean(widened * widened, axis=1, keepdims=True)
-        normed = (widened * lax.rsqrt(mean_square + EPSILON) * norm_gain).astype(jnp.bfloat16)
-        keep = lax.dynamic_slice_in_dim(normed, half * (depth // 2), depth // 2, 1)
-        send = lax.dynamic_slice_in_dim(normed, (1 - half) * (depth // 2), depth // 2, 1)
-        for rows, kept in ((swapped(send, "seq", 2 * near), away_rows), (keep, own_rows)):
-            layers = [rows if o == 0 else swapped(rows, "seq", 2 * o) for o in range(near)]
-            rows = lax.all_gather(jnp.stack(layers), "chan", axis=1, tiled=True)
-            kept.append(rows.reshape(near * part_rows, depth // 2))
+        for j in range(PARTS):
+            add_partial(i, j)
 
     short = lax.dynamic_slice_in_dim(short_taps, place * mine, mine, 2)
     skip = lax.dynamic_slice_in_dim(skip_gain, place * mine, mine, 0).reshape(1, mine)
@@ -201,15 +322,8 @@
     far = [(2 * i + 1, 2 * (near + i)) for i in range(near)]
     gates = []
     for i in range(pieces):
-        sums = []
-        for j in range(PARTS):
-            sent = project(order, away_rows[j], sections[i], None)
-            sums.append(swapped(sent, "seq", 2 * near))
-        sums = [
-            project(order, own_rows[j], sections[i], sums[j]).reshape(near, part_rows, 3 * width)
-            for j in range(PARTS)
-        ]
-        edge = sums[-1][:, part_rows - EDGE :]
+        joined = [value.reshape(near, part_rows, 3 * width) for value in sums[i]]
+        edge = joined[-1][:, part_rows - EDGE :]
         edge = jnp.stack([lax.dynamic_index_in_dim(edge, place ^ o, 0, False) for o in range(near)])
         across = swapped(edge, "seq", 1)
         before = jnp.concatenate([lax.ppermute(edge[-1:], "seq", far), across[:-1]], 0)
@@ -218,7 +332,7 @@
         span = slice(i * width, (i + 1) * width)
         gated = gate(
             halo,
-            sums,
+            joined,
             short[:, :, span].reshape(3, 3 * width),
             skip[:, span],
             toeplitz[:, i * some : (i + 1) * some].reshape(TAPS, some * 2 * TAPS),

time: 527 us -> 610 us (1.16)
  waiting for transfers between devices: 241 us -> 322 us
  local copies, waits for them, and re-layouts: 63.5 us -> 88.6 us
  blocking collectives: 17 us -> 0 us
  between operations: 14.6 us -> 1.45 us
    ppermute x37 -> x55, waiting for transfers between devices: 229 us -> 322 us  [swapped(): lax.ppermute(value, axis, [(i, i ^ bit) for i in range(lax.axis_size(axis...]
    optimization_barrier x0 -> x14, local copies, waits for them, and re-layouts: none -> 28.9 us  [the longest x4 9.17 us: per_device(): moved, own_rows, own_pair, nears = hold((moved, own_rows, own_pair, nears))]
    all_to_all x1 -> x0, blocking collectives: 17 us -> none  [per_device(): widened = lax.all_to_all(part, 'chan', 0, 1, tiled=True).astype(jnp.float32)]
    all_to_all x1 -> x0, waiting for transfers between devices: 12.6 us -> none  [per_device(): widened = lax.all_to_all(part, 'chan', 0, 1, tiled=True).astype(jnp.float32)]
    reshape x8 -> x3, local copies, waits for them, and re-layouts: 14.3 us -> 2.34 us  [the longest x2 2.34 us: cut(): lax.dynamic_slice_in_dim(w_in, start, width, 2)]
    unnamed x93 -> x141, local copies, waits for them, and re-layouts: 37 us -> 47.1 us
    concatenate x0 -> x8, other arithmetic: none -> 7.46 us  [the longest x4 4.92 us: near_rows(): jnp.concatenate([rows if o == 0 else swapped(rows, 'seq', 2 * o) for o in...]
    ppermute x37 -> x55, starting transfers between devices: 47.8 us -> 47.4 us  [swapped(): lax.ppermute(value, axis, [(i, i ^ bit) for i in range(lax.axis_size(axis...]
  transfers between devices with their start and end apart: 46 -> 59, of which waited for: 22 -> 21; matrix products, arithmetic and copies ran while one was open for 11% -> 12% of each run, Pallas kernels for 19% -> 14%
where the time goes in v3:
time: 610 us; the launch traced here: 599 us
  waiting for transfers between devices  322 us (53%)
  Pallas kernels  106 us (17%)
  local copies, waits for them, and re-layouts  88.6 us (15%)
  starting transfers between devices  59.5 us (10%)
  other arithmetic  17.6 us (3%)
    ppermute x55, waiting for transfers between devices, swapped(): lax.ppermute(value, axis, [(i, i ^ bit) for i in range(lax.axis_size(axis...  322 us
    pallas_call x16, Pallas kernels, project(): pl.pallas_call(kernel, in_specs=[smem, smem] + [vmem] * (ranks + len(sect...  80.3 us
    ppermute x55, starting transfers between devices, swapped(): lax.ppermute(value, axis, [(i, i ^ bit) for i in range(lax.axis_size(axis...  47.4 us
    unnamed x141, local copies, waits for them, and re-layouts  47.1 us
    pallas_call x4, Pallas kernels, out_block(): pl.pallas_call(kernel, grid_spec=pltpu.PrefetchScalarGridSpec(num_scalar_...  19.1 us
  transfers between devices with their start and end apart: 59, of which 21 were waited for; matrix products, arithmetic and copies ran while one was open for 12% of the time, Pallas kernels for 14%

profile of v3, /device:TPU:4, one launch (start us, length us, event | category | flops | bytes accessed | tf_op | source)
XLA Modules:
  0.0 598.7 jit_solution(8198964150539318210)
XLA Ops:
  0.0 5.2 constant_dynamic-slice_fusion.28
  39.5 6.5 %collective-permute-done.7 = bf16[64,2048]{1,0:T(8,128)(2,1)S(1)} collective-permute-done((bf16[64,2048]{1,0:T(8,128)(2,1)S(1)}, bf16[64,2048]{1,0:T(8,128)(2,1)S(1)}, u32[]{:S(2)}, u32[]{:S(2)}) %collective-permute-start.7) | collective-permute-done | bytes 262176 | tf_op jit(solution)/shard_map/ppermute | solution.py:16
  50.7 9.3 %collective-permute-done.5 = bf16[64,4096]{1,0:T(8,128)(2,1)} collective-permute-done((bf16[64,4096]{1,0:T(8,128)(2,1)S(1)}, bf16[64,4096]{1,0:T(8,128)(2,1)}, u32[]{:S(2)}, u32[]{:S(2)}) %collective-permute-start.5) | collective-permute-done | bytes 524320 | tf_op jit(solution)/shard_map/ppermute | solution.py:16
  69.3 17.4 %collective-permute-done.10 = bf16[64,4096]{1,0:T(8,128)(2,1)} collective-permute-done((bf16[64,4096]{1,0:T(8,128)(2,1)}, bf16[64,4096]{1,0:T(8,128)(2,1)}, u32[]{:S(2)}, u32[]{:S(2)}) %collective-permute-start.10) | collective-permute-done | bytes 524320 | tf_op jit(solution)/shard_map/ppermute | solution.py:16
  89.6 14.0 %collective-permute-done.13.refs_6_ = bf16[1024,384]{1,0:T(8,128)(2,1)} collective-permute-done((bf16[1024,384]{1,0:T(8,128)(2,1)}, bf16[1024,384]{1,0:T(8,128)(2,1)}, u32[]{:S(2)}, u32[]{:S(2)}) %collective-permute-start.13) | collective-permute-done | bytes 786464 | tf_op jit(solution)/shard_map/ppermute | solution.py:16
  105.1 22.7 %collective-permute-done.16.refs_2_ = bf16[128,4096]{1,0:T(8,128)(2,1)S(1)} collective-permute-done((bf16[128,4096]{1,0:T(8,128)(2,1)S(1)}, bf16[128,4096]{1,0:T(8,128)(2,1)S(1)}, u32[]{:S(2)}, u32[]{:S(2)}) %collective-permute-start.16) | collective-permute-done | bytes 1048608 | tf_op jit(solution)/shard_map/ppermute | solution.py:16
  131.8 11.1 %collective-permute-done.14 = bf16[64,4096]{1,0:T(8,128)(2,1)} collective-permute-done((bf16[64,4096]{1,0:T(8,128)(2,1)}, bf16[64,4096]{1,0:T(8,128)(2,1)}, u32[]{:S(2)}, u32[]{:S(2)}) %collective-permute-start.14) | collective-permute-done | bytes 524320 | tf_op jit(solution)/shard_map/ppermute | solution.py:16
  144.2 15.2 %collective-permute-done.19.refs_6_ = bf16[1024,384]{1,0:T(8,128)(2,1)} collective-permute-done((bf16[1024,384]{1,0:T(8,128)(2,1)}, bf16[1024,384]{1,0:T(8,128)(2,1)}, u32[]{:S(2)}, u32[]{:S(2)}) %collective-permute-start.19) | collective-permute-done | bytes 786464 | tf_op jit(solution)/shard_map/ppermute | solution.py:16
  161.7 23.4 %collective-permute-done.22.refs_2_ = bf16[128,4096]{1,0:T(8,128)(2,1)} collective-permute-done((bf16[128,4096]{1,0:T(8,128)(2,1)S(1)}, bf16[128,4096]{1,0:T(8,128)(2,1)}, u32[]{:S(2)}, u32[]{:S(2)}) %collective-permute-start.22) | collective-permute-done | bytes 1048608 | tf_op jit(solution)/shard_map/ppermute | solution.py:16
  205.4 19.0 %collective-permute-done.20.refs_8_ = bf16[512,384]{1,0:T(8,128)(2,1)S(1)} collective-permute-done((bf16[512,384]{1,0:T(8,128)(2,1)S(1)}, bf16[512,384]{1,0:T(8,128)(2,1)S(1)}, u32[]{:S(2)}, u32[]{:S(2)}) %collective-permute-start.20) | collective-permute-done | bytes 393248 | tf_op jit(solution)/shard_map/ppermute | solution.py:16
  226.8 23.2 %collective-permute-done.30.refs_2_ = bf16[128,4096]{1,0:T(8,128)(2,1)} collective-permute-done((bf16[128,4096]{1,0:T(8,128)(2,1)S(1)}, bf16[128,4096]{1,0:T(8,128)(2,1)}, u32[]{:S(2)}, u32[]{:S(2)}) %collective-permute-start.30) | collective-permute-done | bytes 1048608 | tf_op jit(solution)/shard_map/ppermute | solution.py:16
  257.9 5.2 project.18
  278.8 14.3 %collective-permute-done.28.refs_8_ = bf16[512,384]{1,0:T(8,128)(2,1)} collective-permute-done((bf16[512,384]{1,0:T(8,128)(2,1)}, bf16[512,384]{1,0:T(8,128)(2,1)}, u32[]{:S(2)}, u32[]{:S(2)}) %collective-permute-start.28) | collective-permute-done | bytes 393248 | tf_op jit(solution)/shard_map/ppermute | solution.py:16
  293.0 7.4 %collective-permute-done.27.refs_8_ = bf16[512,384]{1,0:T(8,128)(2,1)S(1)} collective-permute-done((bf16[512,384]{1,0:T(8,128)(2,1)S(1)}, bf16[512,384]{1,0:T(8,128)(2,1)S(1)}, u32[]{:S(2)}, u32[]{:S(2)}) %collective-permute-start.27) | collective-permute-done | bytes 393248 | tf_op jit(solution)/shard_map/ppermute | solution.py:16
  302.8 22.9 %collective-permute-done.37.refs_2_ = bf16[128,4096]{1,0:T(8,128)(2,1)} collective-permute-done((bf16[128,4096]{1,0:T(8,128)(2,1)S(1)}, bf16[128,4096]{1,0:T(8,128)(2,1)}, u32[]{:S(2)}, u32[]{:S(2)}) %collective-permute-start.37) | collective-permute-done | bytes 1048608 | tf_op jit(solution)/shard_map/ppermute | solution.py:16
  333.8 5.0 project.20
  339.0 4.9 project.19
  350.5 18.1 %collective-permute-done.35.refs_8_ = bf16[512,384]{1,0:T(8,128)(2,1)S(1)} collective-permute-done((bf16[512,384]{1,0:T(8,128)(2,1)S(1)}, bf16[512,384]{1,0:T(8,128)(2,1)S(1)}, u32[]{:S(2)}, u32[]{:S(2)}) %collective-permute-start.35) | collective-permute-done | bytes 393248 | tf_op jit(solution)/shard_map/ppermute | solution.py:16
  369.4 7.0 %collective-permute-done.34.refs_8_ = bf16[512,384]{1,0:T(8,128)(2,1)S(1)} collective-permute-done((bf16[512,384]{1,0:T(8,128)(2,1)S(1)}, bf16[512,384]{1,0:T(8,128)(2,1)S(1)}, u32[]{:S(2)}, u32[]{:S(2)}) %collective-permute-start.34) | collective-permute-done | bytes 393248 | tf_op jit(solution)/shard_map/ppermute | solution.py:16
  391.1 6.0 %project.21 = bf16[512,384]{1,0:T(8,128)(2,1)} custom-call(s32[4]{0:T(128)S(1)} %get-tuple-element.337.order_ref, s32[4]{0:T(128)S(1)} %get-tuple-element.338.places_ref, bf16[128,4096]{1,0:T(8,128)(2,1)S(1)} %copy-done.4, bf16[128,4096]{1,0:T(8,128)(2,1)} %collective-permute-done.21.refs_1_, bf16[128,4096]{1,0:T(8,128)(2,1)} %collective-permute-done.22.refs_2_, ...), custom_call_target="tpu_custom_call" | custom-call | flops 1610612736 | bytes 7733248 | tf_op jit(solution)/shard_map/project/pallas_call | solution.py:48
  404.0 12.1 %collective-permute-done.40.refs_8_ = bf16[512,384]{1,0:T(8,128)(2,1)} collective-permute-done((bf16[512,384]{1,0:T(8,128)(2,1)}, bf16[512,384]{1,0:T(8,128)(2,1)}, u32[]{:S(2)}, u32[]{:S(2)}) %collective-permute-start.40) | collective-permute-done | bytes 393248 | tf_op jit(solution)/shard_map/ppermute | solution.py:16
  418.4 4.9 project.30
  423.3 5.4 project.28
  428.8 4.9 project.22
  443.6 5.3 project.26
  454.3 4.9 project.25
  459.2 5.2 project.27
  475.5 27.0 %collective-permute-done.48.refs_8_ = bf16[512,384]{1,0:T(8,128)(2,1)S(1)} collective-permute-done((bf16[512,384]{1,0:T(8,128)(2,1)S(1)}, bf16[512,384]{1,0:T(8,128)(2,1)S(1)}, u32[]{:S(2)}, u32[]{:S(2)}) %collective-permute-start.48) | collective-permute-done | bytes 393248 | tf_op jit(solution)/shard_map/ppermute | solution.py:16
  502.5 5.2 project.29
  512.6 6.9 %collective-permute-start.50 = (bf16[1,144,384]{2,1,0:T(8,128)(2,1)S(1)}, bf16[1,144,384]{2,1,0:T(8,128)(2,1)S(1)}, u32[]{:S(2)}, u32[]{:S(2)}) collective-permute-start(bf16[1,144,384]{2,1,0:T(8,128)(2,1)S(1)} %get-tuple-element.316), channel_id=1, source_target_pairs={{4,16},{12,24},{5,17},{13,25},{6,18},{14,26},{7,19},{15,27}} | collective-permute-start | bytes 331784 | tf_op jit(solution)/shard_map/ppermute | solution.py:329
  519.5 5.2 project.31
  554.0 41.3 %collective-permute-done.57 = bf16[512,2048]{1,0:T(8,128)(2,1)S(1)} collective-permute-done((bf16[512,2048]{1,0:T(8,128)(2,1)S(1)}, bf16[512,2048]{1,0:T(8,128)(2,1)S(1)}, u32[]{:S(2)}, u32[]{:S(2)}) %collective-permute-start.57) | collective-permute-done | bytes 2097184 | tf_op jit(solution)/shard_map/ppermute | solution.py:16
  (338 shorter events, 211.6 us)
Async XLA Ops:
  28.1 31.9 %collective-permute-start.9 = (bf16[1024,384]{1,0:T(8,128)(2,1)S(1)}, bf16[1024,384]{1,0:T(8,128)(2,1)S(1)}, u32[]{:S(2)}, u32[]{:S(2)}) collective-permute-start(bf16[1024,384]{1,0:T(8,128)(2,1)S(1)} %collective-permute-done.4.refs_6_), channel_id=1, source_target_pairs={{0,4},{4,0},{8,12},{12,8},{16,20},{20,16},{24,28},{28,24},{1,5},{5... | collective-permute-start | bytes 2359304 | tf_op jit(solution)/shard_map/ppermute | solution.py:16
  34.0 26.0 %collective-permute-start.5 = (bf16[64,4096]{1,0:T(8,128)(2,1)S(1)}, bf16[64,4096]{1,0:T(8,128)(2,1)}, u32[]{:S(2)}, u32[]{:S(2)}) collective-permute-start(bf16[64,4096]{1,0:T(8,128)(2,1)S(1)} %pad_maximum_fusion.7), channel_id=1, source_target_pairs={{0,16},{4,20},{8,24},{12,28},{16,0},{20,4},{24,8},{28,12},{1,17},{... | collective-permute-start | bytes 1572872 | tf_op jit(solution)/shard_map/ppermute | solution.py:16
  61.3 25.4 %collective-permute-start.10 = (bf16[64,4096]{1,0:T(8,128)(2,1)}, bf16[64,4096]{1,0:T(8,128)(2,1)}, u32[]{:S(2)}, u32[]{:S(2)}) collective-permute-start(bf16[64,4096]{1,0:T(8,128)(2,1)} %collective-permute-done.5), channel_id=1, source_target_pairs={{0,8},{4,12},{8,0},{12,4},{16,24},{20,28},{24,16},{28,20},{1,9},{5... | collective-permute-start | bytes 1572872 | tf_op jit(solution)/shard_map/ppermute | solution.py:16
  62.2 26.4 %collective-permute-start.11 = (bf16[64,4096]{1,0:T(8,128)(2,1)}, bf16[64,4096]{1,0:T(8,128)(2,1)}, u32[]{:S(2)}, u32[]{:S(2)}) collective-permute-start(bf16[64,4096]{1,0:T(8,128)(2,1)} %pad_maximum_fusion.9), channel_id=1, source_target_pairs={{0,16},{4,20},{8,24},{12,28},{16,0},{20,4},{24,8},{28,12},{1,17},{... | collective-permute-start | bytes 1572872 | tf_op jit(solution)/shard_map/ppermute | solution.py:16
  68.4 35.2 %collective-permute-start.13 = (bf16[1024,384]{1,0:T(8,128)(2,1)}, bf16[1024,384]{1,0:T(8,128)(2,1)}, u32[]{:S(2)}, u32[]{:S(2)}) collective-permute-start(bf16[1024,384]{1,0:T(8,128)(2,1)} %copy.27), channel_id=1, source_target_pairs={{0,8},{4,12},{8,0},{12,4},{16,24},{20,28},{24,16},{28,20},{1,9},{5... | collective-permute-start | bytes 2359304 | tf_op jit(solution)/shard_map/ppermute | solution.py:16
  105.1 55.1 %collective-permute-start.15 = (bf16[128,4096]{1,0:T(8,128)(2,1)S(1)}, bf16[128,4096]{1,0:T(8,128)(2,1)}, u32[]{:S(2)}, u32[]{:S(2)}) collective-permute-start(bf16[128,4096]{1,0:T(8,128)(2,1)S(1)} %pad_maximum_fusion.2.refs_0_), channel_id=1, source_target_pairs={{0,1},{1,0},{2,3},{3,2},{4,5},{5,4},{6,7},{7,6},{8,9},{9,8},{10,11... | collective-permute-start | bytes 3145736 | tf_op jit(solution)/shard_map/ppermute | solution.py:16
  127.8 32.4 %collective-permute-start.17 = (bf16[128,4096]{1,0:T(8,128)(2,1)S(1)}, bf16[128,4096]{1,0:T(8,128)(2,1)}, u32[]{:S(2)}, u32[]{:S(2)}) collective-permute-start(bf16[128,4096]{1,0:T(8,128)(2,1)S(1)} %collective-permute-done.16.refs_2_), channel_id=1, source_target_pairs={{0,1},{1,0},{2,3},{3,2},{4,5},{5,4},{6,7},{7,6},{8,9},{9,8},{10,11... | collective-permute-start | bytes 3145736 | tf_op jit(solution)/shard_map/ppermute | solution.py:16
  129.7 29.7 %collective-permute-start.19 = (bf16[1024,384]{1,0:T(8,128)(2,1)}, bf16[1024,384]{1,0:T(8,128)(2,1)}, u32[]{:S(2)}, u32[]{:S(2)}) collective-permute-start(bf16[1024,384]{1,0:T(8,128)(2,1)} %copy.28), channel_id=1, source_target_pairs={{0,8},{4,12},{8,0},{12,4},{16,24},{20,28},{24,16},{28,20},{1,9},{5... | collective-permute-start | bytes 2359304 | tf_op jit(solution)/shard_map/ppermute | solution.py:16
  131.1 28.3 %collective-permute-start.18 = (bf16[1024,384]{1,0:T(8,128)(2,1)}, bf16[1024,384]{1,0:T(8,128)(2,1)S(1)}, u32[]{:S(2)}, u32[]{:S(2)}) collective-permute-start(bf16[1024,384]{1,0:T(8,128)(2,1)} %collective-permute-done.13.refs_6_), channel_id=1, source_target_pairs={{0,4},{4,0},{8,12},{12,8},{16,20},{20,16},{24,28},{28,24},{1,5},{5... | collective-permute-start | bytes 2359304 | tf_op jit(solution)/shard_map/ppermute | solution.py:16
  160.2 24.9 %collective-permute-start.22 = (bf16[128,4096]{1,0:T(8,128)(2,1)S(1)}, bf16[128,4096]{1,0:T(8,128)(2,1)}, u32[]{:S(2)}, u32[]{:S(2)}) collective-permute-start(bf16[128,4096]{1,0:T(8,128)(2,1)S(1)} %pad_maximum_fusion.3.refs_0_), channel_id=1, source_target_pairs={{0,2},{1,3},{2,0},{3,1},{4,6},{5,7},{6,4},{7,5},{8,10},{9,11},{10,... | collective-permute-start | bytes 3145736 | tf_op jit(solution)/shard_map/ppermute | solution.py:16
  161.7 63.4 %collective-permute-start.21 = (bf16[128,4096]{1,0:T(8,128)(2,1)S(1)}, bf16[128,4096]{1,0:T(8,128)(2,1)}, u32[]{:S(2)}, u32[]{:S(2)}) collective-permute-start(bf16[128,4096]{1,0:T(8,128)(2,1)S(1)} %pad_maximum_fusion.3.refs_0_), channel_id=1, source_target_pairs={{0,1},{1,0},{2,3},{3,2},{4,5},{5,4},{6,7},{7,6},{8,9},{9,8},{10,11... | collective-permute-start | bytes 3145736 | tf_op jit(solution)/shard_map/ppermute | solution.py:16
  185.1 40.0 %collective-permute-start.23 = (bf16[128,4096]{1,0:T(8,128)(2,1)}, bf16[128,4096]{1,0:T(8,128)(2,1)}, u32[]{:S(2)}, u32[]{:S(2)}) collective-permute-start(bf16[128,4096]{1,0:T(8,128)(2,1)} %collective-permute-done.22.refs_2_), channel_id=1, source_target_pairs={{0,1},{1,0},{2,3},{3,2},{4,5},{5,4},{6,7},{7,6},{8,9},{9,8},{10,11... | collective-permute-start | bytes 3145736 | tf_op jit(solution)/shard_map/ppermute | solution.py:16
  188.1 37.0 %collective-permute-start.25 = (bf16[1024,384]{1,0:T(8,128)(2,1)}, bf16[1024,384]{1,0:T(8,128)(2,1)}, u32[]{:S(2)}, u32[]{:S(2)}) collective-permute-start(bf16[1024,384]{1,0:T(8,128)(2,1)} %copy.30), channel_id=1, source_target_pairs={{0,4},{4,0},{8,12},{12,8},{16,20},{20,16},{24,28},{28,24},{1,5},{5... | collective-permute-start | bytes 2359304 | tf_op jit(solution)/shard_map/ppermute | solution.py:16
  191.2 34.0 %collective-permute-start.26 = (bf16[1024,384]{1,0:T(8,128)(2,1)}, bf16[1024,384]{1,0:T(8,128)(2,1)}, u32[]{:S(2)}, u32[]{:S(2)}) collective-permute-start(bf16[1024,384]{1,0:T(8,128)(2,1)} %copy.31), channel_id=1, source_target_pairs={{0,8},{4,12},{8,0},{12,4},{16,24},{20,28},{24,16},{28,20},{1,9},{5... | collective-permute-start | bytes 2359304 | tf_op jit(solution)/shard_map/ppermute | solution.py:16
  225.2 24.8 %collective-permute-start.30 = (bf16[128,4096]{1,0:T(8,128)(2,1)S(1)}, bf16[128,4096]{1,0:T(8,128)(2,1)}, u32[]{:S(2)}, u32[]{:S(2)}) collective-permute-start(bf16[128,4096]{1,0:T(8,128)(2,1)S(1)} %pad_maximum_fusion.4.refs_0_), channel_id=1, source_target_pairs={{0,2},{1,3},{2,0},{3,1},{4,6},{5,7},{6,4},{7,5},{8,10},{9,11},{10,... | collective-permute-start | bytes 3145736 | tf_op jit(solution)/shard_map/ppermute | solution.py:16
  226.8 74.4 %collective-permute-start.29 = (bf16[128,4096]{1,0:T(8,128)(2,1)S(1)}, bf16[128,4096]{1,0:T(8,128)(2,1)}, u32[]{:S(2)}, u32[]{:S(2)}) collective-permute-start(bf16[128,4096]{1,0:T(8,128)(2,1)S(1)} %pad_maximum_fusion.4.refs_0_), channel_id=1, source_target_pairs={{0,1},{1,0},{2,3},{3,2},{4,5},{5,4},{6,7},{7,6},{8,9},{9,8},{10,11... | collective-permute-start | bytes 3145736 | tf_op jit(solution)/shard_map/ppermute | solution.py:16
  250.0 51.2 %collective-permute-start.31 = (bf16[128,4096]{1,0:T(8,128)(2,1)}, bf16[128,4096]{1,0:T(8,128)(2,1)}, u32[]{:S(2)}, u32[]{:S(2)}) collective-permute-start(bf16[128,4096]{1,0:T(8,128)(2,1)} %collective-permute-done.30.refs_2_), channel_id=1, source_target_pairs={{0,1},{1,0},{2,3},{3,2},{4,5},{5,4},{6,7},{7,6},{8,9},{9,8},{10,11... | collective-permute-start | bytes 3145736 | tf_op jit(solution)/shard_map/ppermute | solution.py:16
  250.0 26.5 %collective-permute-start.32 = (bf16[64,4096]{1,0:T(8,128)(2,1)}, bf16[64,4096]{1,0:T(8,128)(2,1)}, u32[]{:S(2)}, u32[]{:S(2)}) collective-permute-start(bf16[64,4096]{1,0:T(8,128)(2,1)} %pad_maximum_fusion.8), channel_id=1, source_target_pairs={{0,8},{4,12},{8,0},{12,4},{16,24},{20,28},{24,16},{28,20},{1,9},{5... | collective-permute-start | bytes 1572872 | tf_op jit(solution)/shard_map/ppermute | solution.py:16
  250.2 51.0 %collective-permute-start.33 = (bf16[1024,384]{1,0:T(8,128)(2,1)}, bf16[1024,384]{1,0:T(8,128)(2,1)}, u32[]{:S(2)}, u32[]{:S(2)}) collective-permute-start(bf16[1024,384]{1,0:T(8,128)(2,1)} %collective-permute-done.19.refs_6_), channel_id=1, source_target_pairs={{0,4},{4,0},{8,12},{12,8},{16,20},{20,16},{24,28},{28,24},{1,5},{5... | collective-permute-start | bytes 2359304 | tf_op jit(solution)/shard_map/ppermute | solution.py:16
  263.1 30.0 %collective-permute-start.28 = (bf16[512,384]{1,0:T(8,128)(2,1)}, bf16[512,384]{1,0:T(8,128)(2,1)}, u32[]{:S(2)}, u32[]{:S(2)}) collective-permute-start(bf16[512,384]{1,0:T(8,128)(2,1)} %project.18), channel_id=1, source_target_pairs={{0,16},{4,20},{8,24},{12,28},{16,0},{20,4},{24,8},{28,12},{1,17},{... | collective-permute-start | bytes 1179656 | tf_op jit(solution)/shard_map/ppermute | solution.py:16
  302.8 74.3 %collective-permute-start.36 = (bf16[128,4096]{1,0:T(8,128)(2,1)S(1)}, bf16[128,4096]{1,0:T(8,128)(2,1)}, u32[]{:S(2)}, u32[]{:S(2)}) collective-permute-start(bf16[128,4096]{1,0:T(8,128)(2,1)S(1)} %pad_maximum_fusion.5.refs_0_), channel_id=1, source_target_pairs={{0,1},{1,0},{2,3},{3,2},{4,5},{5,4},{6,7},{7,6},{8,9},{9,8},{10,11... | collective-permute-start | bytes 3145736 | tf_op jit(solution)/shard_map/ppermute | solution.py:16
  325.6 51.5 %collective-permute-start.38 = (bf16[128,4096]{1,0:T(8,128)(2,1)}, bf16[128,4096]{1,0:T(8,128)(2,1)}, u32[]{:S(2)}, u32[]{:S(2)}) collective-permute-start(bf16[128,4096]{1,0:T(8,128)(2,1)} %collective-permute-done.37.refs_2_), channel_id=1, source_target_pairs={{0,1},{1,0},{2,3},{3,2},{4,5},{5,4},{6,7},{7,6},{8,9},{9,8},{10,11... | collective-permute-start | bytes 3145736 | tf_op jit(solution)/shard_map/ppermute | solution.py:16
  327.9 49.2 %collective-permute-start.39 = (bf16[1024,384]{1,0:T(8,128)(2,1)}, bf16[1024,384]{1,0:T(8,128)(2,1)}, u32[]{:S(2)}, u32[]{:S(2)}) collective-permute-start(bf16[1024,384]{1,0:T(8,128)(2,1)} %copy.36), channel_id=1, source_target_pairs={{0,4},{4,0},{8,12},{12,8},{16,20},{20,16},{24,28},{28,24},{1,5},{5... | collective-permute-start | bytes 2359304 | tf_op jit(solution)/shard_map/ppermute | solution.py:16
  338.9 29.8 %collective-permute-start.35 = (bf16[512,384]{1,0:T(8,128)(2,1)S(1)}, bf16[512,384]{1,0:T(8,128)(2,1)S(1)}, u32[]{:S(2)}, u32[]{:S(2)}) collective-permute-start(bf16[512,384]{1,0:T(8,128)(2,1)S(1)} %project.20), channel_id=1, source_target_pairs={{0,16},{4,20},{8,24},{12,28},{16,0},{20,4},{24,8},{28,12},{1,17},{... | collective-permute-start | bytes 1179656 | tf_op jit(solution)/shard_map/ppermute | solution.py:16
  343.9 32.5 %collective-permute-start.34 = (bf16[512,384]{1,0:T(8,128)(2,1)S(1)}, bf16[512,384]{1,0:T(8,128)(2,1)S(1)}, u32[]{:S(2)}, u32[]{:S(2)}) collective-permute-start(bf16[512,384]{1,0:T(8,128)(2,1)S(1)} %project.19), channel_id=1, source_target_pairs={{0,16},{4,20},{8,24},{12,28},{16,0},{20,4},{24,8},{28,12},{1,17},{... | collective-permute-start | bytes 1179656 | tf_op jit(solution)/shard_map/ppermute | solution.py:16
  377.1 38.9 %collective-permute-start.41 = (bf16[1024,384]{1,0:T(8,128)(2,1)}, bf16[1024,384]{1,0:T(8,128)(2,1)}, u32[]{:S(2)}, u32[]{:S(2)}) collective-permute-start(bf16[1024,384]{1,0:T(8,128)(2,1)} %collective-permute-done.26.refs_6_), channel_id=1, source_target_pairs={{0,4},{4,0},{8,12},{12,8},{16,20},{20,16},{24,28},{28,24},{1,5},{5... | collective-permute-start | bytes 2359304 | tf_op jit(solution)/shard_map/ppermute | solution.py:16
  433.7 35.5 %collective-permute-start.43 = (bf16[1,144,384]{2,1,0:T(8,128)(2,1)S(1)}, bf16[1,144,384]{2,1,0:T(8,128)(2,1)S(1)}, u32[]{:S(2)}, u32[]{:S(2)}) collective-permute-start(bf16[1,144,384]{2,1,0:T(8,128)(2,1)S(1)} %get-tuple-element.304), channel_id=1, source_target_pairs={{4,16},{12,24},{5,17},{13,25},{6,18},{14,26},{7,19},{15,27}} | collective-permute-start | bytes 331784 | tf_op jit(solution)/shard_map/ppermute | solution.py:329
  435.9 28.5 %collective-permute-start.42 = (bf16[2,144,384]{2,1,0:T(8,128)(2,1)S(1)}, bf16[2,144,384]{2,1,0:T(8,128)(2,1)S(1)}, u32[]{:S(2)}, u32[]{:S(2)}) collective-permute-start(bf16[2,144,384]{2,1,0:T(8,128)(2,1)S(1)} %pad_maximum_fusion.10), channel_id=1, source_target_pairs={{0,4},{4,0},{8,12},{12,8},{16,20},{20,16},{24,28},{28,24},{1,5},{5... | collective-permute-start | bytes 663560 | tf_op jit(solution)/shard_map/ppermute | solution.py:16
  440.9 28.5 %collective-permute-start.45 = (bf16[1,144,384]{2,1,0:T(8,128)(2,1)S(1)}, bf16[1,144,384]{2,1,0:T(8,128)(2,1)S(1)}, u32[]{:S(2)}, u32[]{:S(2)}) collective-permute-start(bf16[1,144,384]{2,1,0:T(8,128)(2,1)S(1)} %get-tuple-element.308), channel_id=1, source_target_pairs={{4,16},{12,24},{5,17},{13,25},{6,18},{14,26},{7,19},{15,27}} | collective-permute-start | bytes 331784 | tf_op jit(solution)/shard_map/ppermute | solution.py:329
  466.1 46.5 %collective-permute-start.51 = (bf16[512,384]{1,0:T(8,128)(2,1)S(1)}, bf16[512,384]{1,0:T(8,128)(2,1)S(1)}, u32[]{:S(2)}, u32[]{:S(2)}) collective-permute-start(bf16[512,384]{1,0:T(8,128)(2,1)S(1)} %project.30), channel_id=1, source_target_pairs={{0,16},{4,20},{8,24},{12,28},{16,0},{20,4},{24,8},{28,12},{1,17},{... | collective-permute-start | bytes 1179656 | tf_op jit(solution)/shard_map/ppermute | solution.py:16
  466.2 36.3 %collective-permute-start.48 = (bf16[512,384]{1,0:T(8,128)(2,1)S(1)}, bf16[512,384]{1,0:T(8,128)(2,1)S(1)}, u32[]{:S(2)}, u32[]{:S(2)}) collective-permute-start(bf16[512,384]{1,0:T(8,128)(2,1)S(1)} %project.28), channel_id=1, source_target_pairs={{0,16},{4,20},{8,24},{12,28},{16,0},{20,4},{24,8},{28,12},{1,17},{... | collective-permute-start | bytes 1179656 | tf_op jit(solution)/shard_map/ppermute | solution.py:16
  547.6 47.6 %collective-permute-start.57 = (bf16[512,2048]{1,0:T(8,128)(2,1)S(1)}, bf16[512,2048]{1,0:T(8,128)(2,1)S(1)}, u32[]{:S(2)}, u32[]{:S(2)}) collective-permute-start(bf16[512,2048]{1,0:T(8,128)(2,1)S(1)} %add_convert_fusion.1), channel_id=1, source_target_pairs={{0,2},{1,3},{2,0},{3,1},{4,6},{5,7},{6,4},{7,5},{8,10},{9,11},{10,... | collective-permute-start | bytes 6291464 | tf_op jit(solution)/shard_map/ppermute | solution.py:16
  (90 other events, 1423.4 us)
